TPU v7x, 128 devices: a whole 4x4x4 slice. The times are simulated.
128 devices in a mesh: dp: 32 (over x, z, core), group: 4 (over y).
Axes of the slice: x: 4, y: 4, z: 4, core: 2. Of those that a mesh axis runs over, the one named last changes fastest.
Arguments:
- query_inner: bfloat16 [1024, 32, 3072], P(('dp', 'group')), may hold values from -6 to 6
- query_resid: bfloat16 [1024, 32, 768], P(('dp', 'group')), may hold values from -6 to 6
- passage_inner: bfloat16 [1024, 128, 3072], P(('dp', 'group')), may hold values from -6 to 6
- passage_resid: bfloat16 [1024, 128, 768], P(('dp', 'group')), may hold values from -6 to 6
- out_weight: bfloat16 [3072, 768], replicated, may hold values from -0.109375 to 0.109375
- norm_gain: float32 [768], replicated, may hold values from 0.5 to 1.5
- norm_bias: float32 [768], replicated, may hold values from -3 to 3
- proj_weight: bfloat16 [768, 128], replicated, may hold values from -0.21875 to 0.21875
- negative_owner: int32 [1024, 16], P(('dp', 'group')), may hold values from 0 to 127, all different within a row; in each aligned block of 8 rows (0 to 7, 8 to 15, ...) at most 2 rows name the same one
- negative_index: int32 [1024, 16], P(('dp', 'group')), may hold values from 0 to 7, as said below
Outputs:
- query_loss: float32 [1024], P(('dp', 'group'))
- grad_query_inner: bfloat16 [1024, 32, 3072], P(('dp', 'group'))
- grad_query_resid: bfloat16 [1024, 32, 768], P(('dp', 'group'))
- grad_passage_inner: bfloat16 [1024, 128, 3072], P(('dp', 'group'))
- grad_passage_resid: bfloat16 [1024, 128, 768], P(('dp', 'group'))
- grad_out_weight: float32 [3072, 768], replicated
- grad_proj_weight: float32 [768, 128], replicated
- grad_norm: float32 [2, 768], replicated
Inputs may be any that keep to these rules, and one draw needn't show every extreme that they name: `negative_owner`: the 16 negatives of one query lie on 16 different devices. Among the queries of one device, no device is named more than 2 times, and in some device's queries one device is named exactly 2 times. `negative_index`: never equal to the query's own position among its device's 8 queries.
All inputs are finite; a program needn't handle non-finite values.
Results may differ from a plain program's by a relative error of at most 0.015.
Values may be sent and summed in bfloat16 or wider, within the bound.
A program may use at most 192 MiB of HBM per device.

v0:
```python
import jax
import jax.numpy as jnp
from jax import lax
from jax.sharding import PartitionSpec as P

HID = 768
FFW = 3072
DIM = 128
QLEN = 32
PLEN = 128
NEG = 16
Q_DEV = 8


pool_temp = 0.05
loss_scale = 1024.0
norm_eps = 1e-05
unit_eps = 1e-06


def encode(hidden_in, resid_in, out_weight, norm_gain, norm_bias, proj_weight):
    summed = jnp.dot(hidden_in, out_weight, preferred_element_type=jnp.float32) + resid_in.astype(
        jnp.float32
    )
    center = summed - jnp.mean(summed, axis=-1, keepdims=True)
    reciprocal = lax.rsqrt(jnp.mean(center * center, axis=-1, keepdims=True) + norm_eps)
    normed = center * reciprocal
    layer_out = (normed * norm_gain + norm_bias).astype(jnp.bfloat16)
    projected = jnp.dot(layer_out, proj_weight, preferred_element_type=jnp.float32)
    length = jnp.sqrt(jnp.sum(projected * projected, axis=-1, keepdims=True) + unit_eps)
    unit_vec = projected / length
    return ((layer_out, normed, reciprocal, length, unit_vec), unit_vec.astype(jnp.bfloat16))


def encode_back(stored, grad_unit, hidden_in, out_weight, norm_gain, proj_weight):
    layer_out, normed, reciprocal, length, unit_vec = stored
    grad_projected = (
        (grad_unit - unit_vec * jnp.sum(unit_vec * grad_unit, axis=-1, keepdims=True)) / length
    ).astype(jnp.bfloat16)
    weight_proj = jnp.dot(layer_out.T, grad_projected, preferred_element_type=jnp.float32)
    grad_layer = jnp.dot(grad_projected, proj_weight.T, preferred_element_type=jnp.float32)
    norm_grads = jnp.stack([jnp.sum(grad_layer * normed, axis=0), jnp.sum(grad_layer, axis=0)])
    grad_normed = grad_layer * norm_gain
    grad_summed = (
        reciprocal
        * (
            grad_normed
            - jnp.mean(grad_normed, axis=-1, keepdims=True)
            - normed * jnp.mean(grad_normed * normed, axis=-1, keepdims=True)
        )
    ).astype(jnp.bfloat16)
    weight_out = jnp.dot(hidden_in.T, grad_summed, preferred_element_type=jnp.float32)
    grad_hidden = jnp.dot(grad_summed, out_weight.T, preferred_element_type=jnp.float32).astype(
        jnp.bfloat16
    )
    return (grad_hidden, grad_summed, weight_out, weight_proj, norm_grads)


def pool_scores(query_side, passage_side):
    logits = (
        jnp.einsum(
            "...id,...jd->...ij", query_side, passage_side, preferred_element_type=jnp.float32
        )
        / pool_temp
    )
    exp_logits = jnp.exp(logits)
    totals = jnp.sum(exp_logits, axis=-1, keepdims=True)
    pair_score = pool_temp * jnp.sum(jnp.log(totals[..., 0]), axis=-1)
    return (pair_score, (exp_logits / totals).astype(jnp.bfloat16))


def pull_toward(weights, passage_side):
    return jnp.einsum(
        "...ij,...jd->...id", weights, passage_side, preferred_element_type=jnp.float32
    )


def push_toward(weights, query_side):
    return jnp.einsum("...ij,...id->...jd", weights, query_side, preferred_element_type=jnp.float32)


def softmax_loss(scores):
    exp_scores = jnp.exp(scores)
    totals = jnp.sum(exp_scores, axis=-1, keepdims=True)
    query_loss = jnp.log(totals[:, 0]) - scores[:, 0]
    target = (jnp.arange(scores.shape[-1]) == 0).astype(jnp.float32)
    return (query_loss, loss_scale * (exp_scores / totals - target))


def local(
    query_inner,
    query_resid,
    passage_inner,
    passage_resid,
    out_weight,
    norm_gain,
    norm_bias,
    proj_weight,
    negative_owner,
    negative_index,
):
    devices = lax.axis_size(("dp", "group"))
    capacity = max(2, 2 * Q_DEV * NEG // devices)
    slot_total = devices * capacity
    query_flat = query_inner.reshape(Q_DEV * QLEN, FFW)
    passage_flat = passage_inner.reshape(Q_DEV * PLEN, FFW)
    query_stored, query_emb = encode(
        query_flat,
        query_resid.reshape(Q_DEV * QLEN, HID),
        out_weight,
        norm_gain,
        norm_bias,
        proj_weight,
    )
    passage_stored, passage_emb = encode(
        passage_flat,
        passage_resid.reshape(Q_DEV * PLEN, HID),
        out_weight,
        norm_gain,
        norm_bias,
        proj_weight,
    )
    query_emb = query_emb.reshape(Q_DEV, QLEN, DIM)
    passage_emb = passage_emb.reshape(Q_DEV, PLEN, DIM)
    pair_owner = negative_owner.reshape(-1)
    owner_hot = (pair_owner[:, None] == jnp.arange(devices, dtype=jnp.int32)[None, :]).astype(
        jnp.int32
    )
    pair_rank = jnp.sum((jnp.cumsum(owner_hot, axis=0) - owner_hot) * owner_hot, axis=1)
    pair_slot = pair_owner * capacity + pair_rank
    wanted = jnp.full((slot_total,), Q_DEV, jnp.int32).at[pair_slot].set(negative_index.reshape(-1))
    requested = lax.all_to_all(wanted, ("dp", "group"), split_axis=0, concat_axis=0, tiled=True)
    served = jnp.minimum(requested, Q_DEV - 1)
    gather_hot = (
        (served[None, :] == jnp.arange(Q_DEV, dtype=jnp.int32)[:, None])
        & (requested[None, :] < Q_DEV)
    ).astype(jnp.float32)
    anchor_score, anchor_weights = pool_scores(query_emb, passage_emb)
    anchor_pull = pull_toward(anchor_weights, passage_emb)
    anchor_push = push_toward(anchor_weights, query_emb)
    fetched = lax.all_to_all(
        passage_emb[served], ("dp", "group"), split_axis=0, concat_axis=0, tiled=True
    )
    negative_rows = fetched[pair_slot].reshape(Q_DEV, NEG, PLEN, DIM)
    query_wide = jnp.broadcast_to(query_emb[:, None], (Q_DEV, NEG, QLEN, DIM))
    negative_score, negative_weights = pool_scores(query_wide, negative_rows)
    query_loss, seed_grad = softmax_loss(
        jnp.concatenate([anchor_score[:, None], negative_score], axis=1)
    )
    negative_seed = seed_grad[:, 1:, None, None]
    negative_pull = negative_seed * pull_toward(negative_weights, negative_rows)
    negative_push = negative_seed * push_toward(negative_weights, query_wide)
    outgoing = (
        jnp.zeros((slot_total, PLEN, DIM), jnp.float32)
        .at[pair_slot]
        .set(negative_push.reshape(Q_DEV * NEG, PLEN, DIM))
    )
    returned = lax.all_to_all(
        outgoing.astype(jnp.bfloat16), ("dp", "group"), split_axis=0, concat_axis=0, tiled=True
    ).astype(outgoing.dtype)
    query_grad = seed_grad[:, 0, None, None] * anchor_pull + jnp.sum(negative_pull, axis=1)
    remote_push = jnp.dot(
        gather_hot, returned.reshape(slot_total, PLEN * DIM), precision=lax.Precision.HIGHEST
    )
    passage_grad = seed_grad[:, 0, None, None] * anchor_push + remote_push.reshape(Q_DEV, PLEN, DIM)
    query_back = encode_back(
        query_stored,
        query_grad.reshape(Q_DEV * QLEN, DIM),
        query_flat,
        out_weight,
        norm_gain,
        proj_weight,
    )
    passage_back = encode_back(
        passage_stored,
        passage_grad.reshape(Q_DEV * PLEN, DIM),
        passage_flat,
        out_weight,
        norm_gain,
        proj_weight,
    )
    summed_grads = lax.psum(
        (
            query_back[2] + passage_back[2],
            query_back[3] + passage_back[3],
            query_back[4] + passage_back[4],
        ),
        ("dp", "group"),
    )
    return (
        query_loss,
        query_back[0].reshape(Q_DEV, QLEN, FFW),
        query_back[1].reshape(Q_DEV, QLEN, HID),
        passage_back[0].reshape(Q_DEV, PLEN, FFW),
        passage_back[1].reshape(Q_DEV, PLEN, HID),
        summed_grads[0],
        summed_grads[1],
        summed_grads[2],
    )


def solution(mesh):
    in_specs = (
        P(("dp", "group"), None, None),
        P(("dp", "group"), None, None),
        P(("dp", "group"), None, None),
        P(("dp", "group"), None, None),
        P(),
        P(),
        P(),
        P(),
        P(("dp", "group"), None),
        P(("dp", "group"), None),
    )
    out_specs = (
        P(("dp", "group")),
        P(("dp", "group"), None, None),
        P(("dp", "group"), None, None),
        P(("dp", "group"), None, None),
        P(("dp", "group"), None, None),
        P(),
        P(),
        P(),
    )
    return jax.shard_map(local, mesh=mesh, in_specs=in_specs, out_specs=out_specs, check_vma=False)
```

profile of v0, /device:TPU:1, one launch (start us, length us, event | category | flops | bytes accessed | tf_op | source)
XLA Modules:
  0.0 546.5 jit_solution(495290798004527462)
XLA Ops:
  11.8 11.5 %all-to-all-start = ((s32[128,2,1]{1,2,0:T(1,128)}), s32[128,2,1]{1,2,0:T(1,128)S(1)}, u32[]{:S(2)}, u32[]{:S(2)}) async-start(s32[128,2,1]{1,2,0:T(1,128)} %bitcast.9), calls=%async_computation | async-start | bytes 131072 | tf_op jit(solution)/shard_map/all_to_all | solution.py:132
  23.3 8.9 %fusion.28 = (f32[1024]{0:T(1024)S(1)}, f32[1024,768]{1,0:T(8,128)S(1)}) fusion(bf16[1024,768]{1,0:T(8,128)(2,1)} %bitcast.107, bf16[1024,3072]{1,0:T(8,128)(2,1)} %bitcast.103, bf16[3072,768]{1,0:T(8,128)(2,1)} %param.14), kind=kOutput, calls=%fused_computation.98 | convolution fusion | flops 4834196480 | bytes 15732736 | tf_op jit(solution)/shard_map/dot_general | solution.py:22
  37.8 8.5 %gather_fusion = bf16[256,128,128]{2,1,0:T(8,128)(2,1)} fusion(bf16[8,128,128]{2,1,0:T(8,128)(2,1)S(1)} %bitcast.89, s32[1024]{0:T(1024)S(1)} %pad_clamp_fusion.1), kind=kCustom, calls=%fused_computation | custom fusion | bytes 16778240 | tf_op jit(solution)/shard_map/gather | solution.py:142
  46.3 10.9 %all-to-all-start.1 = ((bf16[256,128,128]{2,1,0:T(8,128)(2,1)}), bf16[256,128,128]{2,1,0:T(8,128)(2,1)}, u32[]{:S(2)}, u32[]{:S(2)}) async-start(bf16[256,128,128]{2,1,0:T(8,128)(2,1)} %gather_fusion), calls=%async_computation.1 | async-start | bytes 16777216 | tf_op jit(solution)/shard_map/all_to_all | solution.py:141
  57.2 3.9 fusion.29
  67.8 1.3 copy.33
  69.7 1.3 pad_clamp_fusion
  71.0 90.8 %all-to-all-done.1 = bf16[256,128,128]{2,1,0:T(8,128)(2,1)} async-done(((bf16[256,128,128]{2,1,0:T(8,128)(2,1)}), bf16[256,128,128]{2,1,0:T(8,128)(2,1)}, u32[]{:S(2)}, u32[]{:S(2)}) %all-to-all-start.1) | async-done | bytes 8388640 | tf_op jit(solution)/shard_map/all_to_all | solution.py:141
  161.8 6.6 %gather_fusion.1 = bf16[128,128,128]{2,1,0:T(8,128)(2,1)} fusion(bf16[256,128,128]{2,1,0:T(8,128)(2,1)} %all-to-all-done.1, s32[1024]{0:T(1024)} %pad_clamp_fusion), kind=kCustom, calls=%fused_computation.1 | custom fusion | bytes 8389120 | tf_op jit(solution)/shard_map/gather | solution.py:144
  168.4 4.6 fusion.2
  174.5 5.6 %broadcast_multiply_fusion = f32[8,16,128,128]{3,2,1,0:T(8,128)} fusion(f32[8,16]{1,0:T(8,128)S(1)} %slice.8, bf16[8,32,128]{2,1,0:T(8,128)(2,1)S(1)} %bitcast.99, f32[8,16,32,128]{3,2,1,0:T(8,128)S(1)} %get-tuple-element.61, f32[8,16,32]{2,1,0:T(8,128)S(1)} %get-tuple-element.60), kind=kOutput, calls=%fused_computation.8 | convolution fusion | flops 137887744 | bytes 10568192 | tf_op jit(solution)/shard_map/...ij,...id->...jd/dot_general | solution.py:79
  180.1 7.8 %broadcast_in_dim.5 = f32[256,128,128]{2,1,0:T(8,128)} broadcast(f32[]{:T(128)} %constant.13.clone.1), dimensions={} | broadcast | bytes 16777220 | tf_op jit(solution)/shard_map/broadcast_in_dim | solution.py:154
  187.9 23.6 %scatter_fusion = f32[256,128,128]{2,1,0:T(8,128)} fusion(f32[256,128,128]{2,1,0:T(8,128)} %broadcast_in_dim.5, s32[128]{0:T(128)} %copy-done.44, f32[128,128,128]{2,1,0:T(8,128)} %bitcast.94), kind=kCustom, calls=%fused_computation.3 | custom fusion | bytes 25166336 | tf_op jit(solution)/shard_map/scatter | solution.py:156
  211.6 9.2 %convert_element_type.78 = bf16[256,128,128]{2,1,0:T(8,128)(2,1)} convert(f32[256,128,128]{2,1,0:T(8,128)} %scatter_fusion) | non-fusion elementwise | flops 4194304 | bytes 25165824 | tf_op jit(solution)/shard_map/convert_element_type | solution.py:159
  220.7 6.7 %all-to-all-start.2 = ((bf16[256,128,128]{2,1,0:T(8,128)(2,1)}), bf16[256,128,128]{2,1,0:T(8,128)(2,1)}, u32[]{:S(2)}, u32[]{:S(2)}) async-start(bf16[256,128,128]{2,1,0:T(8,128)(2,1)} %convert_element_type.78), calls=%async_computation.2 | async-start | bytes 16777216 | tf_op jit(solution)/shard_map/all_to_all | solution.py:158
  227.6 1.6 compare_reduce_fusion
  229.3 1.4 lt.41
  230.7 1.5 min.26
  233.1 4.2 multiply_reduce_fusion.4
  240.0 92.1 %all-to-all-done.2 = bf16[256,128,128]{2,1,0:T(8,128)(2,1)} async-done(((bf16[256,128,128]{2,1,0:T(8,128)(2,1)}), bf16[256,128,128]{2,1,0:T(8,128)(2,1)}, u32[]{:S(2)}, u32[]{:S(2)}) %all-to-all-start.2) | async-done | bytes 8388640 | tf_op jit(solution)/shard_map/all_to_all | solution.py:158
  332.2 13.0 %copy.37 = bf16[256,128,128]{0,2,1:T(8,128)(2,1)} copy(bf16[256,128,128]{2,1,0:T(8,128)(2,1)} %all-to-all-done.2) | data formatting | bytes 16777216 | tf_op jit(solution)/shard_map/reshape | solution.py:163
  345.2 5.7 %fusion = f32[8,128,128]{2,0,1:T(8,128)S(1)} fusion(bf16[256,128,128]{0,2,1:T(8,128)(2,1)} %copy.37, s32[256]{0:T(256)S(1)} %copy-done.40, pred[256]{0:T(512)(128)(4,1)S(1)} %copy-done.47), kind=kOutput, calls=%fused_computation.5 | convolution fusion | flops 67112960 | bytes 8914176 | tf_op jit(solution)/shard_map/dot_general | solution.py:162
  352.8 1.9 multiply_reduce_fusion
  354.7 1.1 convolution_add_fusion.1
  355.8 1.2 multiply_convert_fusion
  357.1 5.2 fusion.31
  362.3 5.2 add_bitcast_fusion
  368.8 4.9 convolution_convert_fusion.1
  373.7 63.6 %psum.23 = f32[2,768]{1,0:T(2,128)} all-reduce(f32[2,768]{1,0:T(2,128)S(1)} %maximum_add_fusion), channel_id=1, replica_groups=mesh['dp'=32,'group'=4] {'dp','group'}, use_global_device_ids=true, to_apply=%region_28.29 | all-reduce | flops 1536 | bytes 12288 | tf_op jit(solution)/shard_map/psum | solution.py:182
  437.3 9.3 %convolution_convert_fusion = bf16[1024,3072]{1,0:T(8,128)(2,1)} fusion(bf16[1024,768]{1,0:T(8,128)(2,1)S(1)} %multiply_convert_fusion, bf16[3072,768]{1,0:T(8,128)(2,1)} %param.14), kind=kOutput, calls=%fused_computation.7 | convolution fusion | flops 4834983936 | bytes 12582912 | tf_op jit(solution)/shard_map/dot_general | solution.py:53
  446.6 82.4 %all-reduce.3.cloned.1.call-done = (f32[3072,768]{0,1:T(8,128)}, f32[768,128]{1,0:T(8,128)}) async-done(((f32[3072,768]{0,1:T(8,128)}, f32[768,128]{1,0:T(8,128)}), (f32[3072,768]{0,1:T(8,128)}, f32[768,128]{1,0:T(8,128)})) %all-reduce.3.cloned.1.call-update) | async-done | bytes 9830416 | tf_op jit(solution)/shard_map/psum | solution.py:182
  529.1 9.6 %copy.36 = f32[3072,768]{1,0:T(8,128)} copy(f32[3072,768]{0,1:T(8,128)} %get-tuple-element.48) | data formatting | bytes 18874368
  (170 shorter events, 26.2 us)
Async XLA Ops:
  7.2 50.0 %copy-start = (bf16[8,32,3072]{2,1,0:T(8,128)(2,1)S(1)}, bf16[8,32,3072]{2,1,0:T(8,128)(2,1)}, u32[]{:S(2)}) copy-start(bf16[8,32,3072]{2,1,0:T(8,128)(2,1)} %param.10) | copy-start | bytes 4718596
  10.1 22.2 %copy-start.44 = (s32[128]{0:T(128)}, s32[128]{0:T(128)S(1)}, u32[]{:S(2)}) copy-start(s32[128]{0:T(128)S(1)} %fusion.22) | copy-start | bytes 1540
  11.8 23.8 %all-to-all-start = ((s32[128,2,1]{1,2,0:T(1,128)}), s32[128,2,1]{1,2,0:T(1,128)S(1)}, u32[]{:S(2)}, u32[]{:S(2)}) async-start(s32[128,2,1]{1,2,0:T(1,128)} %bitcast.9), calls=%async_computation | async-start | bytes 131072 | tf_op jit(solution)/shard_map/all_to_all | solution.py:132
  35.6 10.7 %copy-start.19 = (s32[128,2,1]{1,2,0:T(1,128)}, s32[128,2,1]{1,2,0:T(1,128)S(1)}, u32[]{:S(2)}) copy-start(s32[128,2,1]{1,2,0:T(1,128)S(1)} %all-to-all-done) | copy-start | bytes 3076
  46.3 115.5 %all-to-all-start.1 = ((bf16[256,128,128]{2,1,0:T(8,128)(2,1)}), bf16[256,128,128]{2,1,0:T(8,128)(2,1)}, u32[]{:S(2)}, u32[]{:S(2)}) async-start(bf16[256,128,128]{2,1,0:T(8,128)(2,1)} %gather_fusion), calls=%async_computation.1 | async-start | bytes 16777216 | tf_op jit(solution)/shard_map/all_to_all | solution.py:141
  57.2 5.4 copy-start.35
  57.2 6.3 %copy-start.12 = (bf16[768,128]{1,0:T(8,128)(2,1)S(1)}, bf16[768,128]{1,0:T(8,128)(2,1)}, u32[]{:S(2)}) copy-start(bf16[768,128]{1,0:T(8,128)(2,1)} %param.17) | copy-start | bytes 589828
  168.4 4.8 copy-start.29
  168.4 5.0 copy-start.52
  168.4 6.1 %copy-start.17 = (bf16[256,128]{1,0:T(8,128)(2,1)S(1)}, bf16[256,128]{1,0:T(8,128)(2,1)}, u32[]{:S(2)}) copy-start(bf16[256,128]{1,0:T(8,128)(2,1)} %copy-done.16) | copy-start | bytes 196612
  173.0 7.0 %copy-start.10 = (f32[8,16,32,128]{3,2,1,0:T(8,128)}, f32[8,16,32,128]{3,2,1,0:T(8,128)S(1)}, u32[]{:S(2)}) copy-start(f32[8,16,32,128]{3,2,1,0:T(8,128)S(1)} %get-tuple-element.61) | copy-start | bytes 6291460
  173.1 7.0 %copy-start.23 = (f32[8,16,32]{2,1,0:T(8,128)}, f32[8,16,32]{2,1,0:T(8,128)S(1)}, u32[]{:S(2)}) copy-start(f32[8,16,32]{2,1,0:T(8,128)S(1)} %get-tuple-element.60) | copy-start | bytes 49156
  174.5 5.6 %copy-start.43 = (f32[8,16]{1,0:T(8,128)}, f32[8,16]{1,0:T(8,128)S(1)}, u32[]{:S(2)}) copy-start(f32[8,16]{1,0:T(8,128)S(1)} %slice.8) | copy-start | bytes 1540
  220.7 111.4 %all-to-all-start.2 = ((bf16[256,128,128]{2,1,0:T(8,128)(2,1)}), bf16[256,128,128]{2,1,0:T(8,128)(2,1)}, u32[]{:S(2)}, u32[]{:S(2)}) async-start(bf16[256,128,128]{2,1,0:T(8,128)(2,1)} %convert_element_type.78), calls=%async_computation.2 | async-start | bytes 16777216 | tf_op jit(solution)/shard_map/all_to_all | solution.py:158
  227.4 301.6 %all-reduce.3.cloned.1.call-start = ((), (), s32[]{:S(2)}) async-start(), calls=%async_computation.3 | async-start | bytes 19660800 | tf_op jit(solution)/shard_map/psum | solution.py:182
  233.0 4.6 copy-start.37
  233.0 4.9 copy-start.4
  233.0 4.9 copy-start.13
  233.0 4.9 copy-start.31
  233.1 4.9 copy-start.33
  240.0 105.1 %copy-start.40 = (s32[256]{0:T(256)S(1)}, s32[256]{0:T(256)}, u32[]{:S(2)}) copy-start(s32[256]{0:T(256)} %min.26) | copy-start | bytes 3076
  240.0 105.1 %copy-start.47 = (pred[256]{0:T(512)(128)(4,1)S(1)}, pred[256]{0:T(512)(128)(4,1)}, u32[]{:S(2)}) copy-start(pred[256]{0:T(512)(128)(4,1)} %lt.41) | copy-start | bytes 772
  345.2 5.8 %copy-start.18 = (bf16[256,128]{1,0:T(8,128)(2,1)S(1)}, bf16[256,128]{1,0:T(8,128)(2,1)}, u32[]{:S(2)}) copy-start(bf16[256,128]{1,0:T(8,128)(2,1)} %copy-done.16) | copy-start | bytes 196612
  345.2 5.7 %copy-start.21 = (f32[8,32,128]{2,1,0:T(8,128)S(1)}, f32[8,32,128]{2,1,0:T(8,128)}, u32[]{:S(2)}) copy-start(f32[8,32,128]{2,1,0:T(8,128)} %get-tuple-element.63) | copy-start | bytes 393220
  345.2 5.8 %copy-start.27 = (f32[8,32]{1,0:T(8,128)S(1)}, f32[8,32]{1,0:T(8,128)}, u32[]{:S(2)}) copy-start(f32[8,32]{1,0:T(8,128)} %copy-done.25) | copy-start | bytes 3076
  345.2 5.8 %copy-start.46 = (f32[8]{0:T(128)S(1)}, f32[8]{0:T(128)}, u32[]{:S(2)}) copy-start(f32[8]{0:T(128)} %copy-done.45) | copy-start | bytes 100
  345.2 6.2 %copy-start.6 = (f32[1024,128]{1,0:T(8,128)S(1)}, f32[1024,128]{1,0:T(8,128)}, u32[]{:S(2)}) copy-start(f32[1024,128]{1,0:T(8,128)} %copy-done.5) | copy-start | bytes 1572868
  357.1 80.2 %copy-start.15 = (bf16[1024,768]{1,0:T(8,128)(2,1)}, bf16[1024,768]{1,0:T(8,128)(2,1)S(1)}, u32[]{:S(2)}) copy-start(bf16[1024,768]{1,0:T(8,128)(2,1)S(1)} %multiply_convert_fusion) | copy-start | bytes 4718596
  357.1 5.2 copy-start.9
  368.8 4.9 copy-start.42
  368.8 4.9 copy-start.41
  529.0 9.6 %copy-start.22 = (f32[768,128]{1,0:T(8,128)S(1)}, f32[768,128]{1,0:T(8,128)}, u32[]{:S(2)}) copy-start(f32[768,128]{1,0:T(8,128)} %get-tuple-element.76) | copy-start | bytes 1179652
  (27 other events, 40.6 us)
Sparse Core Ops, SparseCore 0:
  367.7 161.3 all-reduce.2
where the time goes:
time: 555 us; the launch traced here: 547 us
  waiting for transfers between devices  265 us (48%)
  local copies, waits for them, and re-layouts  86.7 us (16%)
  matrix products  64.8 us (12%)
  blocking collectives  63.6 us (11%)
  starting transfers between devices  29.3 us (5%)
  other arithmetic  21.8 us (4%)
  between operations  15 us (3%)
    all_to_all x1, waiting for transfers between devices, local(): lax.all_to_all(outgoing.astype(jnp.bfloat16), ('dp', 'group'), split_axis...  92.1 us
    all_to_all x1, waiting for transfers between devices, local(): lax.all_to_all(passage_emb[served], ('dp', 'group'), split_axis=0, concat...  90.8 us
    psum x1, waiting for transfers between devices, local(): lax.psum((query_back[2] + passage_back[2], query_back[3] + passage_back[3...  82.4 us
    psum x1, blocking collectives, local(): lax.psum((query_back[2] + passage_back[2], query_back[3] + passage_back[3...  63.6 us
    scatter x1, local copies, waits for them, and re-layouts, local(): outgoing = jnp.zeros((slot_total, PLEN, DIM), jnp.float32).at[pair_slot]....  23.6 us
    unnamed x112, local copies, waits for them, and re-layouts  17.8 us
    dot_general x2, matrix products, encode_back(): jnp.dot(grad_summed, out_weight.T, preferred_element_type=jnp.float32)  14.2 us
    reshape x1, local copies, waits for them, and re-layouts, local(): returned.reshape(slot_total, PLEN * DIM)  13 us
  transfers between devices with their start and end apart: 4, of which 3 were waited for; matrix products, arithmetic and copies ran while one was open for 9% of the time, Pallas kernels for 0%

commit v1 on v0

--- a/solution.py
+++ b/solution.py
@@ -1,6 +1,8 @@
 import jax
 import jax.numpy as jnp
 from jax import lax
+from jax.experimental import pallas as pl
+from jax.experimental.pallas import tpu as pltpu
 from jax.sharding import PartitionSpec as P
 
 HID = 768
@@ -14,6 +16,7 @@
 
 pool_temp = 0.05
 loss_scale = 1024.0
+MESH = pl.DeviceIdType.MESH
 norm_eps = 1e-05
 unit_eps = 1e-06
 
@@ -85,6 +88,196 @@
     query_loss = jnp.log(totals[:, 0]) - scores[:, 0]
     target = (jnp.arange(scores.shape[-1]) == 0).astype(jnp.float32)
     return (query_loss, loss_scale * (exp_scores / totals - target))
+
+
+AXES = ("x", "y", "z")
+ORDERS = (("x", "y", "z"), ("y", "z", "x"), ("z", "x", "y"), ("x", "y", "z"))
+PARTS = 3
+PART_ROWS = 3072
+SIDE_ROWS = 512
+
+
+def position():
+    dp = lax.axis_index("dp")
+    return {"x": dp // 8, "y": lax.axis_index("group"), "z": (dp // 2) % 4, "core": dp % 2}
+
+
+def device_at(place):
+    return ((place["x"] * 4 + place["z"]) * 2 + place["core"], place["y"])
+
+
+def shifted(place, axis, step):
+    return {**place, axis: (place[axis] + step) % (2 if axis == "core" else 4)}
+
+
+def greet(place):
+    barrier = pltpu.get_barrier_semaphore()
+    peers = [shifted(place, axis, t) for axis in AXES for t in (1, 2, 3)] + [shifted(place, "core", 1)]
+    for peer in peers:
+        pl.semaphore_signal(barrier, inc=1, device_id=device_at(peer), device_id_type=MESH)
+    pl.semaphore_wait(barrier, len(peers))
+
+
+def add_rows(out, out_at, terms, rows, chunk):
+    def body(i, carry):
+        at = pl.multiple_of(i * chunk, chunk)
+        total = None
+        for ref, start in terms:
+            value = ref[pl.ds(pl.multiple_of(start + at, 8), chunk), :].astype(jnp.float32)
+            total = value if total is None else total + value
+        out[pl.ds(pl.multiple_of(out_at + at, 8), chunk), :] = total.astype(out.dtype)
+        return carry
+
+    lax.fori_loop(0, rows // chunk, body, 0)
+
+
+def sum_kernel(
+    grad_ref, side_ref, out_ref, side_out,
+    core_in, held, in1, held1, in2, held2, in3,
+    score_in, sheld, sin1, sheld1, sin2, sheld2, sin3,
+    send_sem, recv_sem,
+):
+    place = position()
+    core = place["core"]
+    greet(place)
+    copies = {}
+
+    def send(phase, part, step, src, dst, peer):
+        copy = pltpu.make_async_remote_copy(
+            src_ref=src, dst_ref=dst,
+            send_sem=send_sem.at[phase, part, step], recv_sem=recv_sem.at[phase, part, step],
+            device_id=device_at(peer), device_id_type=MESH,
+        )
+        copy.start()
+        copies[phase, part, step] = copy
+
+    def bufs(part):
+        if part < PARTS:
+            return dict(
+                src=grad_ref.at[part], core_in=core_in.at[part], held=held.at[part],
+                ins=(in1.at[part], in2.at[part], in3.at[part]),
+                helds=(held1.at[part], held2.at[part]), out=out_ref.at[part], rows=PART_ROWS,
+            )
+        return dict(
+            src=side_ref, core_in=score_in, held=sheld, ins=(sin1, sin2, sin3),
+            helds=(sheld1, sheld2), out=side_out, rows=SIDE_ROWS,
+        )
+
+    every = range(PARTS + 1)
+    other = (core + 1) % 2
+    for part in every:
+        b = bufs(part)
+        send(0, part, 0, b["src"].at[other], b["core_in"], shifted(place, "core", 1))
+    for part in every:
+        b = bufs(part)
+        copies[0, part, 0].wait_recv()
+        add_rows(b["held"], 0, [(b["src"].at[core], 0), (b["core_in"], 0)], b["rows"], 128)
+        rows = b["rows"] // 4
+        axis = ORDERS[part][0]
+        for t in (1, 2, 3):
+            peer = shifted(place, axis, t)
+            at = pl.multiple_of(peer[axis] * rows, rows)
+            send(1, part, t - 1, b["held"].at[pl.ds(at, rows)], b["ins"][0].at[t - 1], peer)
+    for phase in (1, 2, 3):
+        for part in every:
+            b = bufs(part)
+            rows = b["rows"] // 4**phase
+            axis = ORDERS[part][phase - 1]
+            here = b["held"] if phase == 1 else b["helds"][phase - 2]
+            for t in (1, 2, 3):
+                copies[phase, part, t - 1].wait_recv()
+            terms = [(here, place[axis] * rows)] + [(b["ins"][phase - 1].at[t], 0) for t in range(3)]
+            if phase < 3:
+                target, at = b["helds"][phase - 1], 0
+            else:
+                target = b["out"].at[core]
+                at = sum(place[a] * (b["rows"] // 4 ** (n + 1)) for n, a in enumerate(ORDERS[part]))
+            add_rows(target, at, terms, rows, 96 if rows % 96 == 0 else min(rows, 64))
+            if phase < 3:
+                axis = ORDERS[part][phase]
+                rows = rows // 4
+                for t in (1, 2, 3):
+                    peer = shifted(place, axis, t)
+                    start = pl.multiple_of(peer[axis] * rows, rows)
+                    send(phase + 1, part, t - 1, target.at[pl.ds(start, rows)], b["ins"][phase].at[t - 1], peer)
+            else:
+                axis = ORDERS[part][2]
+                block = target.at[pl.ds(pl.multiple_of(at, 8 if part == PARTS else 16), rows)]
+                for t in (1, 2, 3):
+                    send(4, part, t - 1, block, block, shifted(place, axis, t))
+    for phase in (4, 5, 6):
+        for part in every:
+            b = bufs(part)
+            for t in (1, 2, 3):
+                copies[phase, part, t - 1].wait_recv()
+            target = b["out"].at[core]
+            if phase < 6:
+                depth = 6 - phase
+                rows = b["rows"] // 4**depth
+                axis = ORDERS[part][depth - 1]
+                at = sum(
+                    place[a] * (b["rows"] // 4 ** (n + 1)) for n, a in enumerate(ORDERS[part][:depth])
+                )
+                block = target.at[pl.ds(pl.multiple_of(at, 8 if part == PARTS else 16), rows)]
+                for t in (1, 2, 3):
+                    send(phase + 1, part, t - 1, block, block, shifted(place, axis, t))
+            else:
+                send(7, part, 0, target, target, shifted(place, "core", 1))
+    for part in every:
+        copies[7, part, 0].wait_recv()
+    for copy in copies.values():
+        copy.wait_send()
+
+
+def sum_over_devices(grad, side):
+    bf, f32 = jnp.bfloat16, jnp.float32
+    vm = lambda *shape: pltpu.VMEM(shape, bf)
+    vf = lambda *shape: pltpu.VMEM(shape, f32)
+    r = PART_ROWS
+    s = SIDE_ROWS
+    return pl.pallas_call(
+        sum_kernel,
+        out_shape=(
+            jax.ShapeDtypeStruct((PARTS, 2, r, DIM), bf),
+            jax.ShapeDtypeStruct((2, s, DIM), f32),
+        ),
+        in_specs=[pl.BlockSpec(memory_space=pltpu.VMEM)] * 2,
+        out_specs=(pl.BlockSpec(memory_space=pltpu.VMEM),) * 2,
+        scratch_shapes=[
+            vm(PARTS, r, DIM), vm(PARTS, r, DIM), vm(PARTS, 3, r // 4, DIM), vm(PARTS, r // 4, DIM),
+            vm(PARTS, 3, r // 16, DIM), vm(PARTS, r // 16, DIM), vm(PARTS, 3, r // 64, DIM),
+            vf(s, DIM), vf(s, DIM), vf(3, s // 4, DIM), vf(s // 4, DIM),
+            vf(3, s // 16, DIM), vf(s // 16, DIM), vf(3, s // 64, DIM),
+            pltpu.SemaphoreType.DMA((8, PARTS + 1, 3)),
+            pltpu.SemaphoreType.DMA((8, PARTS + 1, 3)),
+        ],
+        compiler_params=pltpu.CompilerParams(
+            collective_id=3, has_side_effects=True, vmem_limit_bytes=48 * 1024 * 1024
+        ),
+        name="grad_sum",
+    )(grad, side)
+
+
+def summed_grads(weight_out, weight_proj, norm_grads):
+    grad = (
+        weight_out.astype(jnp.bfloat16)
+        .reshape(2, FFW // 2, PARTS, 2, DIM)
+        .transpose(2, 0, 3, 1, 4)
+        .reshape(PARTS, 2, PART_ROWS, DIM)
+    )
+    side = jnp.concatenate(
+        [weight_proj, norm_grads.reshape(2 * HID // DIM, DIM),
+         jnp.zeros((2 * SIDE_ROWS - HID - 2 * HID // DIM, DIM), jnp.float32)]
+    ).reshape(2, SIDE_ROWS, DIM)
+    grad, side = sum_over_devices(grad, side)
+    total = (
+        grad.reshape(PARTS, 2, 2, FFW // 2, DIM)
+        .transpose(1, 3, 0, 2, 4)
+        .reshape(FFW, HID)
+        .astype(jnp.float32)
+    )
+    side = side.reshape(2 * SIDE_ROWS, DIM)
+    return total, side[:HID], side[HID : HID + 2 * HID // DIM].reshape(2, HID)
 
 
 def local(
@@ -179,13 +372,10 @@
         norm_gain,
         proj_weight,
     )
-    summed_grads = lax.psum(
-        (
-            query_back[2] + passage_back[2],
-            query_back[3] + passage_back[3],
-            query_back[4] + passage_back[4],
-        ),
-        ("dp", "group"),
+    summed = summed_grads(
+        query_back[2] + passage_back[2],
+        query_back[3] + passage_back[3],
+        query_back[4] + passage_back[4],
     )
     return (
         query_loss,
@@ -193,9 +383,9 @@
         query_back[1].reshape(Q_DEV, QLEN, HID),
         passage_back[0].reshape(Q_DEV, PLEN, FFW),
         passage_back[1].reshape(Q_DEV, PLEN, HID),
-        summed_grads[0],
-        summed_grads[1],
-        summed_grads[2],
+        summed[0],
+        summed[1],
+        summed[2],
     )
 
 

time: 555 us -> 498 us (0.90)
  waiting for transfers between devices: 265 us -> 178 us
  blocking collectives: 63.6 us -> 0 us
  local copies, waits for them, and re-layouts: 86.7 us -> 140 us
  Pallas kernels: 0 us -> 52.8 us
  between operations: 15 us -> 1.74 us
    psum x1 -> x0, waiting for transfers between devices: 82.4 us -> none  [local(): lax.psum((query_back[2] + passage_back[2], query_back[3] + passage_back[3...]
    psum x1 -> x0, blocking collectives: 63.6 us -> none  [local(): lax.psum((query_back[2] + passage_back[2], query_back[3] + passage_back[3...]
    pallas_call x0 -> x1, Pallas kernels: none -> 52.8 us  [sum_over_devices(): pl.pallas_call(sum_kernel, out_shape=(jax.ShapeDtypeStruct((PARTS, 2, r,...]
    convert_element_type x0 -> x2, local copies, waits for them, and re-layouts: none -> 33.6 us  [summed_grads(): total = grad.reshape(PARTS, 2, 2, FFW // 2, DIM).transpose(1, 3, 0, 2, 4)...]
    reshape x0 -> x3, local copies, waits for them, and re-layouts: none -> 24.7 us  [the longest x2 24.1 us: summed_grads(): grad = weight_out.astype(jnp.bfloat16).reshape(2, FFW // 2, PARTS, 2, DIM...]
    unnamed x112 -> x122, local copies, waits for them, and re-layouts: 17.8 us -> 9.49 us
  transfers between devices with their start and end apart: 4 -> 3, of which waited for: 3 -> 2; matrix products, arithmetic and copies ran while one was open for 9% -> 8% of each run, Pallas kernels for 0% -> 0%
where the time goes in v1:
time: 498 us; the launch traced here: 489 us
  waiting for transfers between devices  178 us (36%)
  local copies, waits for them, and re-layouts  140 us (28%)
  matrix products  63.3 us (13%)
  Pallas kernels  52.8 us (11%)
  starting transfers between devices  29.4 us (6%)
  other arithmetic  24.3 us (5%)
    all_to_all x1, waiting for transfers between devices, local(): lax.all_to_all(passage_emb[served], ('dp', 'group'), split_axis=0, concat...  90.9 us
    all_to_all x1, waiting for transfers between devices, local(): lax.all_to_all(outgoing.astype(jnp.bfloat16), ('dp', 'group'), split_axis...  87.2 us
    pallas_call x1, Pallas kernels, sum_over_devices(): pl.pallas_call(sum_kernel, out_shape=(jax.ShapeDtypeStruct((PARTS, 2, r,...  52.8 us
    convert_element_type x2, local copies, waits for them, and re-layouts, summed_grads(): total = grad.reshape(PARTS, 2, 2, FFW // 2, DIM).transpose(1, 3, 0, 2, 4)...  33.6 us
    reshape x2, local copies, waits for them, and re-layouts, summed_grads(): grad = weight_out.astype(jnp.bfloat16).reshape(2, FFW // 2, PARTS, 2, DIM...  24.1 us
    scatter x1, local copies, waits for them, and re-layouts, local(): outgoing = jnp.zeros((slot_total, PLEN, DIM), jnp.float32).at[pair_slot]....  23.7 us
    dot_general x2, matrix products, encode_back(): jnp.dot(hidden_in.T, grad_summed, preferred_element_type=jnp.float32)  15 us
    reshape x1, local copies, waits for them, and re-layouts, local(): returned.reshape(slot_total, PLEN * DIM)  13 us
  transfers between devices with their start and end apart: 3, of which 2 were waited for; matrix products, arithmetic and copies ran while one was open for 8% of the time, Pallas kernels for 0%

profile of v1, /device:TPU:1, one launch (start us, length us, event | category | flops | bytes accessed | tf_op | source)
XLA Modules:
  0.0 489.4 jit_solution(6419571608799826284)
XLA Ops:
  5.3 11.5 %all-to-all-start = ((s32[128,2,1]{1,2,0:T(1,128)}), s32[128,2,1]{1,2,0:T(1,128)S(1)}, u32[]{:S(2)}, u32[]{:S(2)}) async-start(s32[128,2,1]{1,2,0:T(1,128)} %bitcast.9), calls=%async_computation | async-start | bytes 131072 | tf_op jit(solution)/shard_map/all_to_all | solution.py:325
  16.8 8.9 %fusion.29 = (f32[1024]{0:T(1024)S(1)}, f32[1024,768]{1,0:T(8,128)S(1)}) fusion(bf16[1024,768]{1,0:T(8,128)(2,1)} %bitcast.127, bf16[1024,3072]{1,0:T(8,128)(2,1)} %bitcast.119, bf16[3072,768]{1,0:T(8,128)(2,1)} %param.14), kind=kOutput, calls=%fused_computation.101 | convolution fusion | flops 4834196480 | bytes 15732736 | tf_op jit(solution)/shard_map/dot_general | solution.py:25
  31.3 8.5 %gather_fusion = bf16[256,128,128]{2,1,0:T(8,128)(2,1)} fusion(bf16[8,128,128]{2,1,0:T(8,128)(2,1)S(1)} %bitcast.104, s32[1024]{0:T(1024)S(1)} %pad_clamp_fusion.1), kind=kCustom, calls=%fused_computation | custom fusion | bytes 16778240 | tf_op jit(solution)/shard_map/gather | solution.py:335
  39.8 10.9 %all-to-all-start.1 = ((bf16[256,128,128]{2,1,0:T(8,128)(2,1)}), bf16[256,128,128]{2,1,0:T(8,128)(2,1)}, u32[]{:S(2)}, u32[]{:S(2)}) async-start(bf16[256,128,128]{2,1,0:T(8,128)(2,1)} %gather_fusion), calls=%async_computation.1 | async-start | bytes 16777216 | tf_op jit(solution)/shard_map/all_to_all | solution.py:334
  50.7 3.9 fusion.30
  64.3 90.9 %all-to-all-done.1 = bf16[256,128,128]{2,1,0:T(8,128)(2,1)} async-done(((bf16[256,128,128]{2,1,0:T(8,128)(2,1)}), bf16[256,128,128]{2,1,0:T(8,128)(2,1)}, u32[]{:S(2)}, u32[]{:S(2)}) %all-to-all-start.1) | async-done | bytes 8388640 | tf_op jit(solution)/shard_map/all_to_all | solution.py:334
  155.3 6.6 %gather_fusion.1 = bf16[128,128,128]{2,1,0:T(8,128)(2,1)} fusion(bf16[256,128,128]{2,1,0:T(8,128)(2,1)} %all-to-all-done.1, s32[1024]{0:T(1024)} %pad_clamp_fusion), kind=kCustom, calls=%fused_computation.1 | custom fusion | bytes 8389120 | tf_op jit(solution)/shard_map/gather | solution.py:337
  161.9 4.6 fusion.3
  167.9 5.6 %broadcast_multiply_fusion = f32[8,16,128,128]{3,2,1,0:T(8,128)} fusion(f32[8,16]{1,0:T(8,128)S(1)} %slice.14, bf16[8,32,128]{2,1,0:T(8,128)(2,1)S(1)} %bitcast.115, f32[8,16,32,128]{3,2,1,0:T(8,128)S(1)} %get-tuple-element.31, f32[8,16,32]{2,1,0:T(8,128)S(1)} %get-tuple-element.30), kind=kOutput, calls=%fused_computation.10 | convolution fusion | flops 137887744 | bytes 10568192 | tf_op jit(solution)/shard_map/...ij,...id->...jd/dot_general | solution.py:82
  173.5 7.8 %broadcast_in_dim.7 = f32[256,128,128]{2,1,0:T(8,128)} broadcast(f32[]{:T(128)} %constant.13.clone.1), dimensions={} | broadcast | bytes 16777220 | tf_op jit(solution)/shard_map/broadcast_in_dim | solution.py:347
  181.4 23.7 %scatter_fusion = f32[256,128,128]{2,1,0:T(8,128)} fusion(f32[256,128,128]{2,1,0:T(8,128)} %broadcast_in_dim.7, s32[128]{0:T(128)} %copy-done.46, f32[128,128,128]{2,1,0:T(8,128)} %bitcast.110), kind=kCustom, calls=%fused_computation.3 | custom fusion | bytes 25166336 | tf_op jit(solution)/shard_map/scatter | solution.py:349
  205.1 9.2 %convert_element_type.96 = bf16[256,128,128]{2,1,0:T(8,128)(2,1)} convert(f32[256,128,128]{2,1,0:T(8,128)} %scatter_fusion) | non-fusion elementwise | flops 4194304 | bytes 25165824 | tf_op jit(solution)/shard_map/convert_element_type | solution.py:352
  214.3 7.1 %all-to-all-start.2 = ((bf16[256,128,128]{2,1,0:T(8,128)(2,1)}), bf16[256,128,128]{2,1,0:T(8,128)(2,1)}, u32[]{:S(2)}, u32[]{:S(2)}) async-start(bf16[256,128,128]{2,1,0:T(8,128)(2,1)} %convert_element_type.96), calls=%async_computation.2 | async-start | bytes 16777216 | tf_op jit(solution)/shard_map/all_to_all | solution.py:351
  222.0 1.6 compare_reduce_fusion
  223.7 1.4 lt.41
  225.1 1.6 min.26
  227.7 4.5 multiply_reduce_fusion.4
  236.2 2.6 convolution_convert_fusion.1
  238.8 87.2 %all-to-all-done.2 = bf16[256,128,128]{2,1,0:T(8,128)(2,1)} async-done(((bf16[256,128,128]{2,1,0:T(8,128)(2,1)}), bf16[256,128,128]{2,1,0:T(8,128)(2,1)}, u32[]{:S(2)}, u32[]{:S(2)}) %all-to-all-start.2) | async-done | bytes 8388640 | tf_op jit(solution)/shard_map/all_to_all | solution.py:351
  325.9 13.0 %copy.41 = bf16[256,128,128]{0,2,1:T(8,128)(2,1)} copy(bf16[256,128,128]{2,1,0:T(8,128)(2,1)} %all-to-all-done.2) | data formatting | bytes 16777216 | tf_op jit(solution)/shard_map/reshape | solution.py:356
  339.0 5.7 %fusion = f32[8,128,128]{2,0,1:T(8,128)S(1)} fusion(bf16[256,128,128]{0,2,1:T(8,128)(2,1)} %copy.41, s32[256]{0:T(256)S(1)} %copy-done.44, pred[256]{0:T(512)(128)(4,1)S(1)} %copy-done.49), kind=kOutput, calls=%fused_computation.6 | convolution fusion | flops 67112960 | bytes 8914176 | tf_op jit(solution)/shard_map/dot_general | solution.py:355
  346.6 1.4 multiply_reduce_fusion
  349.2 7.0 %convolution_convert_fusion = bf16[1024,3072]{1,0:T(8,128)(2,1)} fusion(bf16[1024,768]{1,0:T(8,128)(2,1)S(1)} %multiply_convert_fusion, bf16[3072,768]{1,0:T(8,128)(2,1)S(1)} %bitcast.126), kind=kOutput, calls=%fused_computation.8 | convolution fusion | flops 4834983936 | bytes 12582912 | tf_op jit(solution)/shard_map/dot_general | solution.py:56
  356.2 7.8 %fusion.32 = f32[768,3072]{1,0:T(8,128)} fusion(bf16[1024,768]{1,0:T(8,128)(2,1)S(1)} %multiply_convert_fusion, bf16[1024,3072]{1,0:T(8,128)(2,1)S(1)} %bitcast.122), kind=kOutput, calls=%fused_computation.104 | convolution fusion | flops 4831838208 | bytes 17301504 | tf_op jit(solution)/shard_map/dot_general | solution.py:55
  364.4 7.2 %fusion.2 = bf16[3072,768]{0,1:T(8,128)(2,1)} fusion(f32[768,3072]{1,0:T(8,128)} %fusion.32, bf16[256,768]{1,0:T(8,128)(2,1)S(1)} %copy-done.17, bf16[256,3072]{1,0:T(8,128)(2,1)S(1)} %bitcast.99), kind=kOutput, calls=%fused_computation.9 | convolution fusion | flops 1212678144 | bytes 16121856 | tf_op jit(solution)/shard_map/dot_general | solution.py:55
  371.6 11.6 %reshape.249 = bf16[2,1536,3,2,128]{1,0,4,3,2:T(2,128)(2,1)} reshape(bf16[3072,768]{0,1:T(8,128)(2,1)} %fusion.2) | data formatting | bytes 9437184 | tf_op jit(solution)/shard_map/reshape | solution.py:264
  383.3 12.5 %copy.39 = bf16[2,1536,3,2,128]{4,1,3,0,2:T(8,128)(2,1)} copy(bf16[2,1536,3,2,128]{1,0,4,3,2:T(2,128)(2,1)} %reshape.249) | data formatting | bytes 9437184 | tf_op jit(solution)/shard_map/reshape | solution.py:264
  396.0 52.8 %grad_sum.1 = (bf16[3,2,3072,128]{3,2,1,0:T(8,128)(2,1)S(1)}, f32[2,512,128]{2,1,0:T(8,128)S(1)}) custom-call(bf16[3,2,3072,128]{3,2,1,0:T(8,128)(2,1)} %bitcast.107, f32[2,512,128]{2,1,0:T(8,128)S(1)} %bitcast.101), custom_call_target="tpu_custom_call" | custom-call | tf_op jit(solution)/shard_map/grad_sum/pallas_call | solution.py:238
  448.8 2.2 copy-done.1
  452.3 3.2 convert_bitcast_fusion
  455.5 20.7 %copy.40 = f32[2,1536,3,2,128]{4,3,2,1,0:T(2,128)} copy(f32[2,1536,3,2,128]{4,1,3,0,2:T(8,128)S(1)} %convert_bitcast_fusion) | data formatting | bytes 18874368 | tf_op jit(solution)/shard_map/convert_element_type | solution.py:277
  476.2 13.0 %reshape.256 = f32[3072,768]{1,0:T(8,128)} reshape(f32[2,1536,3,2,128]{4,3,2,1,0:T(2,128)} %copy.40) | data formatting | bytes 18874368 | tf_op jit(solution)/shard_map/convert_element_type | solution.py:277
  (191 shorter events, 31.5 us)
Async XLA Ops:
  0.6 50.1 %copy-start = (bf16[8,32,3072]{2,1,0:T(8,128)(2,1)S(1)}, bf16[8,32,3072]{2,1,0:T(8,128)(2,1)}, u32[]{:S(2)}) copy-start(bf16[8,32,3072]{2,1,0:T(8,128)(2,1)} %param.10) | copy-start | bytes 4718596
  3.5 22.2 %copy-start.46 = (s32[128]{0:T(128)}, s32[128]{0:T(128)S(1)}, u32[]{:S(2)}) copy-start(s32[128]{0:T(128)S(1)} %fusion.23) | copy-start | bytes 1540
  5.3 23.8 %all-to-all-start = ((s32[128,2,1]{1,2,0:T(1,128)}), s32[128,2,1]{1,2,0:T(1,128)S(1)}, u32[]{:S(2)}, u32[]{:S(2)}) async-start(s32[128,2,1]{1,2,0:T(1,128)} %bitcast.9), calls=%async_computation | async-start | bytes 131072 | tf_op jit(solution)/shard_map/all_to_all | solution.py:325
  29.1 10.7 %copy-start.23 = (s32[128,2,1]{1,2,0:T(1,128)}, s32[128,2,1]{1,2,0:T(1,128)S(1)}, u32[]{:S(2)}) copy-start(s32[128,2,1]{1,2,0:T(1,128)S(1)} %all-to-all-done) | copy-start | bytes 3076
  39.8 115.5 %all-to-all-start.1 = ((bf16[256,128,128]{2,1,0:T(8,128)(2,1)}), bf16[256,128,128]{2,1,0:T(8,128)(2,1)}, u32[]{:S(2)}, u32[]{:S(2)}) async-start(bf16[256,128,128]{2,1,0:T(8,128)(2,1)} %gather_fusion), calls=%async_computation.1 | async-start | bytes 16777216 | tf_op jit(solution)/shard_map/all_to_all | solution.py:334
  50.7 5.3 %copy-start.38 = (f32[768]{0:T(1024)S(1)}, f32[768]{0:T(1024)}, u32[]{:S(2)}) copy-start(f32[768]{0:T(1024)} %param.16) | copy-start | bytes 9220
  50.7 6.3 %copy-start.12 = (bf16[768,128]{1,0:T(8,128)(2,1)S(1)}, bf16[768,128]{1,0:T(8,128)(2,1)}, u32[]{:S(2)}) copy-start(bf16[768,128]{1,0:T(8,128)(2,1)} %param.17) | copy-start | bytes 589828
  161.9 6.0 %copy-start.19 = (bf16[256,128]{1,0:T(8,128)(2,1)S(1)}, bf16[256,128]{1,0:T(8,128)(2,1)}, u32[]{:S(2)}) copy-start(bf16[256,128]{1,0:T(8,128)(2,1)} %copy-done.18) | copy-start | bytes 196612
  166.5 7.0 %copy-start.10 = (f32[8,16,32,128]{3,2,1,0:T(8,128)}, f32[8,16,32,128]{3,2,1,0:T(8,128)S(1)}, u32[]{:S(2)}) copy-start(f32[8,16,32,128]{3,2,1,0:T(8,128)S(1)} %get-tuple-element.31) | copy-start | bytes 6291460
  166.5 7.0 %copy-start.26 = (f32[8,16,32]{2,1,0:T(8,128)}, f32[8,16,32]{2,1,0:T(8,128)S(1)}, u32[]{:S(2)}) copy-start(f32[8,16,32]{2,1,0:T(8,128)S(1)} %get-tuple-element.30) | copy-start | bytes 49156
  167.9 5.6 %copy-start.45 = (f32[8,16]{1,0:T(8,128)}, f32[8,16]{1,0:T(8,128)S(1)}, u32[]{:S(2)}) copy-start(f32[8,16]{1,0:T(8,128)S(1)} %slice.14) | copy-start | bytes 1540
  214.3 111.7 %all-to-all-start.2 = ((bf16[256,128,128]{2,1,0:T(8,128)(2,1)}), bf16[256,128,128]{2,1,0:T(8,128)(2,1)}, u32[]{:S(2)}, u32[]{:S(2)}) async-start(bf16[256,128,128]{2,1,0:T(8,128)(2,1)} %convert_element_type.96), calls=%async_computation.2 | async-start | bytes 16777216 | tf_op jit(solution)/shard_map/all_to_all | solution.py:351
  226.7 9.6 %slice-start.2 = ((s8[4718592]{0:T(1024)(128)(4,1)}), s8[4194304]{0:T(1024)(128)(4,1)S(1)}, s32[]{:S(2)}) async-start(s8[4718592]{0:T(1024)(128)(4,1)} %bitcast.123), calls=%async_computation.5 | async-start | bytes 8388608
  227.7 7.0 %copy-start.51 = (f32[8]{0:T(128)S(1)}, f32[8]{0:T(128)}, u32[]{:S(2)}) copy-start(f32[8]{0:T(128)} %copy-done.50) | copy-start | bytes 100
  227.7 7.0 %copy-start.53 = (f32[8]{0:T(128)S(1)}, f32[8]{0:T(128)}, u32[]{:S(2)}) copy-start(f32[8]{0:T(128)} %copy-done.52) | copy-start | bytes 100
  227.7 8.5 %slice-start.3 = ((s8[4718592]{0:T(1024)(128)(4,1)}), s8[524288]{0:T(1024)(128)(4,1)S(1)}, s32[]{:S(2)}) async-start(s8[4718592]{0:T(1024)(128)(4,1)} %bitcast.123), calls=%async_computation.6 | async-start | bytes 1048576
  238.8 100.2 %copy-start.44 = (s32[256]{0:T(256)S(1)}, s32[256]{0:T(256)}, u32[]{:S(2)}) copy-start(s32[256]{0:T(256)} %min.26) | copy-start | bytes 3076
  238.8 100.2 %copy-start.49 = (pred[256]{0:T(512)(128)(4,1)S(1)}, pred[256]{0:T(512)(128)(4,1)}, u32[]{:S(2)}) copy-start(pred[256]{0:T(512)(128)(4,1)} %lt.41) | copy-start | bytes 772
  338.9 5.7 %copy-start.20 = (bf16[256,128]{1,0:T(8,128)(2,1)S(1)}, bf16[256,128]{1,0:T(8,128)(2,1)}, u32[]{:S(2)}) copy-start(bf16[256,128]{1,0:T(8,128)(2,1)} %copy-done.18) | copy-start | bytes 196612
  338.9 5.7 %copy-start.25 = (f32[8,32,128]{2,1,0:T(8,128)S(1)}, f32[8,32,128]{2,1,0:T(8,128)}, u32[]{:S(2)}) copy-start(f32[8,32,128]{2,1,0:T(8,128)} %get-tuple-element.33) | copy-start | bytes 393220
  339.0 5.8 %copy-start.30 = (f32[8,32]{1,0:T(8,128)S(1)}, f32[8,32]{1,0:T(8,128)}, u32[]{:S(2)}) copy-start(f32[8,32]{1,0:T(8,128)} %copy-done.28) | copy-start | bytes 3076
  339.0 5.8 %copy-start.48 = (f32[8]{0:T(128)S(1)}, f32[8]{0:T(128)}, u32[]{:S(2)}) copy-start(f32[8]{0:T(128)} %copy-done.47) | copy-start | bytes 100
  339.0 6.2 %copy-start.7 = (f32[1024,128]{1,0:T(8,128)S(1)}, f32[1024,128]{1,0:T(8,128)}, u32[]{:S(2)}) copy-start(f32[1024,128]{1,0:T(8,128)} %copy-done.6) | copy-start | bytes 1572868
  348.0 8.1 %slice-start = ((s8[6291456]{0:T(1024)(128)(4,1)}), s8[4194304]{0:T(1024)(128)(4,1)S(1)}, s32[]{:S(2)}) async-start(s8[6291456]{0:T(1024)(128)(4,1)} %bitcast.120), calls=%async_computation.3 | async-start | bytes 8388608
  349.2 7.0 %copy-start.15 = (bf16[1024,768]{1,0:T(8,128)(2,1)}, bf16[1024,768]{1,0:T(8,128)(2,1)S(1)}, u32[]{:S(2)}) copy-start(bf16[1024,768]{1,0:T(8,128)(2,1)S(1)} %multiply_convert_fusion) | copy-start | bytes 4718596
  349.2 7.0 %slice-start.1 = ((s8[6291456]{0:T(1024)(128)(4,1)}), s8[2097152]{0:T(1024)(128)(4,1)S(1)}, s32[]{:S(2)}) async-start(s8[6291456]{0:T(1024)(128)(4,1)} %bitcast.120), calls=%async_computation.4 | async-start | bytes 4194304
  356.2 7.8 %copy-start.9 = (bf16[256,768]{1,0:T(8,128)(2,1)S(1)}, bf16[256,768]{1,0:T(8,128)(2,1)}, u32[]{:S(2)}) copy-start(bf16[256,768]{1,0:T(8,128)(2,1)} %copy-done.8) | copy-start | bytes 1179652
  356.2 7.8 %copy-start.22 = (bf16[256,128]{1,0:T(8,128)(2,1)S(1)}, bf16[256,128]{1,0:T(8,128)(2,1)}, u32[]{:S(2)}) copy-start(bf16[256,128]{1,0:T(8,128)(2,1)} %copy-done.21) | copy-start | bytes 196612
  356.2 8.1 %copy-start.42 = (f32[1,768]{1,0:T(1,128)S(1)}, f32[1,768]{1,0:T(1,128)}, u32[]{:S(2)}) copy-start(f32[1,768]{1,0:T(1,128)} %stack.18) | copy-start | bytes 9220
  356.2 8.1 %copy-start.43 = (f32[1,768]{1,0:T(1,128)S(1)}, f32[1,768]{1,0:T(1,128)}, u32[]{:S(2)}) copy-start(f32[1,768]{1,0:T(1,128)} %stack.19) | copy-start | bytes 9220
  356.2 8.2 %copy-start.17 = (bf16[256,768]{1,0:T(8,128)(2,1)S(1)}, bf16[256,768]{1,0:T(8,128)(2,1)}, u32[]{:S(2)}) copy-start(bf16[256,768]{1,0:T(8,128)(2,1)} %copy-done.16) | copy-start | bytes 1179652
  383.3 12.5 %copy-start.41 = (f32[1024]{0:T(1024)S(1)}, f32[1024]{0:T(1024)}, u32[]{:S(2)}) copy-start(f32[1024]{0:T(1024)} %pad.2.clone) | copy-start | bytes 12292
  (32 other events, 77.0 us)

commit v2 on v1

v2 whole, which is shorter than its diff:
```python
import functools

import jax
import jax.numpy as jnp
from jax import lax
from jax.experimental import pallas as pl
from jax.experimental.pallas import tpu as pltpu
from jax.sharding import PartitionSpec as P

HID = 768
FFW = 3072
DIM = 128
QLEN = 32
PLEN = 128
NEG = 16
Q_DEV = 8
DEVICES = 128
CAP = 2
Q_ROWS = Q_DEV * QLEN
P_ROWS = Q_DEV * PLEN
ROWS = Q_ROWS + P_ROWS
CHUNK = 256
SLOTS = DEVICES * CAP
BLOCKS = SLOTS // 8 + Q_DEV
SORTED = BLOCKS * 8
WIDE = 384

MESH = pl.DeviceIdType.MESH
MIB = 1024 * 1024
bf16 = jnp.bfloat16
f32 = jnp.float32

pool_temp = 0.05
loss_scale = 1024.0
norm_eps = 1e-05
unit_eps = 1e-06

AXES = ("x", "y", "z")
ORDERS = (("x", "y", "z"), ("y", "z", "x"), ("z", "x", "y"), ("x", "y", "z"))
PARTS = 3
PART_ROWS = 3072
SIDE_ROWS = 512


def position():
    dp = lax.axis_index("dp")
    return {"x": dp // 8, "y": lax.axis_index("group"), "z": (dp // 2) % 4, "core": dp % 2}


def device_at(place):
    return ((place["x"] * 4 + place["z"]) * 2 + place["core"], place["y"])


def number_of(place):
    return place["x"] * 32 + place["z"] * 8 + place["core"] * 4 + place["y"]


def shifted(place, axis, step):
    return {**place, axis: (place[axis] + step) % (2 if axis == "core" else 4)}


def offset(place, t, sign):
    return {
        "x": (place["x"] + sign * (t // 32) + 4) % 4,
        "z": (place["z"] + sign * ((t // 8) % 4) + 4) % 4,
        "core": (place["core"] + sign * ((t // 4) % 2) + 2) % 2,
        "y": (place["y"] + sign * (t % 4) + 4) % 4,
    }


def dot(a, b, contract):
    return lax.dot_general(a, b, ((contract[:1], contract[1:]), ((), ())), preferred_element_type=f32)


def iota(shape, axis):
    return lax.broadcasted_iota(jnp.int32, shape, axis)


def count_of(mask, axis):
    return jnp.sum(jnp.where(mask, 1, 0), axis=axis, keepdims=True)


def pair_table(codes):
    passage = codes % 16
    sub = iota((SLOTS, 1), 0)
    slot = 2 * (sub % DEVICES) + sub // DEVICES
    square0, square1 = iota((SLOTS, SLOTS), 0), iota((SLOTS, SLOTS), 1)
    passage_row = jnp.sum(jnp.where(square0 == square1, passage, 0), axis=0, keepdims=True)
    rank = count_of((passage_row == passage) & (square1 < square0), 1)
    lane = iota((1, DIM), 1)
    blocks = jnp.where(lane < Q_DEV, (count_of(passage == lane, 0) + 7) // 8, 0)
    start = jnp.sum(jnp.where(lane < passage, blocks, 0), axis=1, keepdims=True)
    place = jnp.where(passage < Q_DEV, start * 8 + rank, SORTED)
    wide = iota((1, WIDE), 1)
    hit = (place == wide) & (wide < SORTED)
    order = jnp.sum(jnp.where(hit, slot - SLOTS, 0), axis=0, keepdims=True) + SLOTS
    order_sub = jnp.sum(jnp.where(hit, sub - SLOTS, 0), axis=0, keepdims=True) + SLOTS
    place_row = jnp.sum(jnp.where(slot == wide, place, 0), axis=0, keepdims=True)
    owner = jnp.zeros((1, WIDE), jnp.int32)
    goes_on = jnp.ones((1, WIDE), jnp.int32)
    last = jnp.zeros((1, WIDE), jnp.int32)
    for p in range(Q_DEV):
        begin = jnp.sum(jnp.where(lane < p, blocks, 0), axis=1, keepdims=True)
        end = jnp.sum(jnp.where(lane <= p, blocks, 0), axis=1, keepdims=True)
        owner += jnp.where(wide >= end, 1, 0)
        goes_on -= jnp.where((wide == begin) & (end > begin), 1, 0)
        last += jnp.where(wide == p, jnp.where(end > begin, end - 1, BLOCKS), 0)
    owner = jnp.minimum(owner, Q_DEV - 1)
    return jnp.concatenate([order, order_sub, place_row, owner, goes_on, last, last, last], axis=0)


def pool(query_side, passage_side):
    exp_logits = jnp.exp(dot(query_side, passage_side, (1, 1)) * (1.0 / pool_temp))
    totals = jnp.sum(exp_logits, axis=1, keepdims=True)
    weights = (exp_logits / totals).astype(bf16)
    queries = query_side.shape[0] // QLEN
    logs = jnp.broadcast_to(jnp.log(totals), (queries * QLEN, DIM)).reshape(queries, QLEN, DIM)
    return weights, pool_temp * jnp.sum(logs, axis=1)


def pair_kernel(
    slot_query, slot_of, codes,
    query_inner, query_resid, passage_inner, passage_resid, out_weight, gain, bias, proj,
    normed_out, unit_out, scale_out, grad_out, loss_out,
    inner, resid, weight, query_emb, passage_emb, codes_in, table, table_s,
    asks_out, asks_in, sorted_q, sorted_w, sorted_pull, sorted_exp, slot_exp, slot_seed, block_seed, chain,
    pulls_out, pulls_in, anchor_w, anchor_pull, anchor_score,
    sums, sums_in1, sums_in2,
    load_sem, table_sem, code_send, code_recv, ask_send, ask_recv, pull_send, pull_recv, sum_send, sum_recv,
):
    place = position()
    me = number_of(place)
    lane_row = iota((1, DIM), 1)

    loads = [
        pltpu.make_async_copy(out_weight, weight, load_sem.at[0]),
        pltpu.make_async_copy(query_inner, inner.at[pl.ds(0, Q_ROWS)], load_sem.at[1]),
        pltpu.make_async_copy(query_resid, resid.at[pl.ds(0, Q_ROWS)], load_sem.at[2]),
        pltpu.make_async_copy(passage_inner, inner.at[pl.ds(Q_ROWS, P_ROWS)], load_sem.at[3]),
        pltpu.make_async_copy(passage_resid, resid.at[pl.ds(Q_ROWS, P_ROWS)], load_sem.at[4]),
    ]
    for load in loads:
        load.start()

    barrier = pltpu.get_barrier_semaphore()

    def greet(t, carry):
        pl.semaphore_signal(barrier, inc=1, device_id=device_at(offset(place, t, 1)), device_id_type=MESH)
        return carry

    lax.fori_loop(1, DEVICES, greet, 0)
    asks_in[SLOTS] = jnp.zeros((QLEN, DIM), bf16)
    sorted_pull[SORTED] = jnp.zeros((QLEN, DIM), bf16)
    sorted_exp[SORTED] = jnp.zeros((1, DIM), f32)
    slot_seed[SLOTS] = jnp.zeros((1, DIM), f32)
    chain[BLOCKS] = jnp.zeros((PLEN, DIM), f32)
    codes_in[0] = codes[0]
    pl.semaphore_wait(barrier, DEVICES - 1)

    def code_copy(t):
        return pltpu.make_async_remote_copy(
            src_ref=codes.at[t], dst_ref=codes_in.at[t], send_sem=code_send, recv_sem=code_recv,
            device_id=device_at(offset(place, t, 1)), device_id_type=MESH,
        )

    def send_code(t, carry):
        code_copy(t).start()
        return carry

    lax.fori_loop(1, DEVICES, send_code, 0)

    def encode(at):
        at = pl.multiple_of(at, CHUNK)
        here = pl.ds(at, CHUNK)
        summed = dot(inner[here, :], weight[...], (1, 0)) + resid[here, :].astype(f32)
        center = summed - jnp.mean(summed, axis=1, keepdims=True)
        reciprocal = lax.rsqrt(jnp.mean(center * center, axis=1, keepdims=True) + norm_eps)
        normed = center * reciprocal
        normed_out[here, :] = normed
        layer_out = (normed * gain[...] + bias[...]).astype(bf16)
        projected = dot(layer_out, proj[...], (1, 0))
        length = jnp.sqrt(jnp.sum(projected * projected, axis=1, keepdims=True) + unit_eps)
        unit = projected / length
        unit_out[here, :] = unit
        scale_out[here, :] = jnp.where(iota((CHUNK, DIM), 1) < DIM // 2, reciprocal, length)
        return unit.astype(bf16)

    for load in loads[:3]:
        load.wait()
    query_emb[...] = encode(0).reshape(Q_DEV, QLEN, DIM)

    def ask_copy(t):
        rows = pl.ds(t * CAP, CAP)
        return pltpu.make_async_remote_copy(
            src_ref=asks_out.at[rows], dst_ref=asks_in.at[rows], send_sem=ask_send, recv_sem=ask_recv,
            device_id=device_at(offset(place, t, 1)), device_id_type=MESH,
        )

    def take_query(s):
        return query_emb[slot_query[s]]

    for r in range(CAP):
        asks_in[r] = take_query(r)

    def send_ask(t, carry):
        for r in range(CAP):
            asks_out[t * CAP + r] = take_query(t * CAP + r)
        ask_copy(t).start()
        return carry

    lax.fori_loop(1, DEVICES, send_ask, 0)

    for load in loads[3:]:
        load.wait()

    def encode_passages(i, carry):
        passages = encode((i + 1) * CHUNK).reshape(CHUNK // PLEN, PLEN, DIM)
        passage_emb[pl.ds(i * (CHUNK // PLEN), CHUNK // PLEN)] = passages
        return carry

    lax.fori_loop(0, P_ROWS // CHUNK, encode_passages, 0)

    rest = pl.ds(1, DEVICES - 1)
    everyone = pltpu.make_async_remote_copy(
        src_ref=codes.at[rest], dst_ref=codes_in.at[rest], send_sem=code_send, recv_sem=code_recv,
        device_id=device_at(offset(place, 1, 1)), device_id_type=MESH,
    )
    everyone.wait()
    code_rows = codes_in[...].reshape(DEVICES, DIM)
    slot_codes = jnp.concatenate([code_rows[:, r : r + 1] for r in range(CAP)], axis=0)
    table[...] = pair_table(slot_codes)
    to_scalar = pltpu.make_async_copy(table, table_s, table_sem)
    to_scalar.start()

    def anchor(i, carry):
        rows = pl.ds(pl.multiple_of(i * QLEN, QLEN), QLEN)
        passage = passage_emb[i]
        weights, score = pool(query_emb[i], passage)
        anchor_w[rows, :] = weights
        anchor_pull[rows, :] = dot(weights, passage, (1, 0))
        anchor_score[pl.ds(i, 1), :] = score
        return carry

    lax.fori_loop(0, Q_DEV, anchor, 0)
    to_scalar.wait()

    def asked(buffer):
        return buffer.at[pl.ds(CAP, (DEVICES - 1) * CAP)]

    all_asks = pltpu.make_async_remote_copy(
        src_ref=asked(asks_out), dst_ref=asked(asks_in), send_sem=ask_send, recv_sem=ask_recv,
        device_id=device_at(offset(place, 1, 1)), device_id_type=MESH,
    )
    all_asks.wait()

    def score_block(b, carry):
        at = pl.multiple_of(b * CHUNK, CHUNK)
        for k in range(8):
            asking = asks_in[table_s[0, b * 8 + k]]
            sorted_q[pl.ds(pl.multiple_of(at + k * QLEN, QLEN), QLEN), :] = asking
        passage = passage_emb[table_s[3, b]]
        weights, score = pool(sorted_q[pl.ds(at, CHUNK), :], passage)
        sorted_w[pl.ds(at, CHUNK), :] = weights
        exp_score = jnp.exp(score)
        sorted_exp[pl.ds(b * 8, 8)] = exp_score.reshape(8, 1, DIM)
        pull = dot(weights, passage, (1, 0)).reshape(8, QLEN, DIM) * exp_score.reshape(8, 1, DIM)
        sorted_pull[pl.ds(b * 8, 8)] = pull.astype(bf16)
        return carry

    lax.fori_loop(0, BLOCKS, score_block, 0)

    def exp_of(t, carry):
        for r in range(CAP):
            slot_exp[pl.ds(r * DEVICES + t, 1), :] = sorted_exp[table_s[2, t * CAP + r]]
        return carry

    lax.fori_loop(0, DEVICES, exp_of, 0)

    t_col = iota((DEVICES, 1), 0)
    source = (
        ((place["x"] + 4 - t_col // 32) % 4) * 32
        + ((place["z"] + 4 - (t_col // 8) % 4) % 4) * 8
        + ((place["core"] + 2 - (t_col // 4) % 2) % 2) * 4
        + (place["y"] + 4 - t_col % 4) % 4
    )
    from_device = source == iota((DEVICES, DEVICES), 1)
    query_index = [(slot_codes[r * DEVICES : (r + 1) * DEVICES] // 16).astype(f32) for r in range(CAP)]
    eight = iota((Q_DEV, DIM), 0).astype(f32)
    own_exp = jnp.exp(anchor_score[...])
    spread = jnp.where(iota((Q_DEV, DIM), 1) == me, own_exp, 0.0)
    for r in range(CAP):
        exps = slot_exp[pl.ds(r * DEVICES, DEVICES), :]
        exp_row = jnp.sum(jnp.where(from_device, exps, 0.0), axis=0, keepdims=True)
        index_row = jnp.sum(jnp.where(from_device, query_index[r], 0.0), axis=0, keepdims=True)
        spread += jnp.where(eight == index_row, exp_row, 0.0)
    sums[0] = spread
    near, far = [], []
    for t in range(1, 8):
        peer = shifted(shifted(place, "core", t // 4), "y", t % 4)
        near.append(pltpu.make_async_remote_copy(
            src_ref=sums.at[0], dst_ref=sums_in1.at[t - 1], send_sem=sum_send.at[t - 1],
            recv_sem=sum_recv.at[t - 1], device_id=device_at(peer), device_id_type=MESH,
        ))
    for t in range(1, 16):
        peer = shifted(shifted(place, "x", t // 4), "z", t % 4)
        far.append(pltpu.make_async_remote_copy(
            src_ref=sums.at[1], dst_ref=sums_in2.at[t - 1], send_sem=sum_send.at[t + 6],
            recv_sem=sum_recv.at[t + 6], device_id=device_at(peer), device_id_type=MESH,
        ))
    for copy in near:
        copy.start()

    def pull_copy(t):
        rows = pl.ds(t * CAP, CAP)
        return pltpu.make_async_remote_copy(
            src_ref=pulls_out.at[rows], dst_ref=pulls_in.at[rows], send_sem=pull_send, recv_sem=pull_recv,
            device_id=device_at(offset(place, t, -1)), device_id_type=MESH,
        )

    def take_pull(s):
        return sorted_pull[table_s[2, s]]

    for copy in near:
        copy.wait_recv()
    sums[1] = sums[0] + jnp.sum(sums_in1[...], axis=0)
    for copy in far:
        copy.start()

    for r in range(CAP):
        pulls_in[r] = take_pull(r)

    def send_pull(t, carry):
        for r in range(CAP):
            pulls_out[t * CAP + r] = take_pull(t * CAP + r)
        pull_copy(t).start()
        return carry

    lax.fori_loop(1, DEVICES, send_pull, 0)
    for copy in far:
        copy.wait_recv()
    total = sums[1] + jnp.sum(sums_in2[...], axis=0)

    for r in range(CAP):
        mine = jnp.zeros((DEVICES, DIM), f32)
        for i in range(Q_DEV):
            mine += jnp.where(from_device & (query_index[r] == float(i)), total[i : i + 1, :], 0.0)
        slot_total = jnp.sum(mine, axis=1, keepdims=True)
        here = pl.ds(r * DEVICES, DEVICES)
        slot_seed[here] = (loss_scale * (slot_exp[here, :] / slot_total)).reshape(DEVICES, 1, DIM)

    def push_block(b, carry):
        at = pl.multiple_of(b * CHUNK, CHUNK)
        for k in range(8):
            block_seed[pl.ds(k, 1), :] = slot_seed[table_s[1, b * 8 + k]]
        seeds = block_seed[...].reshape(8, 1, DIM)
        weights = sorted_w[pl.ds(at, CHUNK), :].astype(f32).reshape(8, QLEN, DIM) * seeds
        push = dot(weights.reshape(CHUNK, DIM).astype(bf16), sorted_q[pl.ds(at, CHUNK), :], (0, 0))
        goes_on = table_s[4, b].astype(f32)
        carry = carry * goes_on + push
        chain[b] = carry
        return carry

    lax.fori_loop(0, BLOCKS, push_block, jnp.zeros((PLEN, DIM), f32))

    own_total = jnp.sum(jnp.where(iota((Q_DEV, DIM), 1) == me, total, 0.0), axis=1, keepdims=True)
    own_total = jnp.broadcast_to(own_total, (Q_DEV, DIM))
    anchor_seed = loss_scale * (own_exp / own_total - 1.0)
    loss_out[...] = jnp.log(own_total) - anchor_score[...]
    for p in range(Q_DEV):
        push = dot(anchor_w[pl.ds(p * QLEN, QLEN), :], query_emb[p], (0, 0)) * anchor_seed[p : p + 1, :]
        push += chain[table_s[5, p]]
        grad_out[pl.ds(Q_ROWS + p * PLEN, PLEN), :] = push

    pltpu.make_async_remote_copy(
        src_ref=asked(pulls_out), dst_ref=asked(pulls_in), send_sem=pull_send, recv_sem=pull_recv,
        device_id=device_at(offset(place, 1, 1)), device_id_type=MESH,
    ).wait()
    query_scale = loss_scale / own_total
    for i in range(Q_DEV):
        rows = pl.ds(i * QLEN, QLEN)
        pull = jnp.zeros((QLEN, DIM), f32)
        for k in range(NEG):
            pull += pulls_in[slot_of[i * NEG + k]].astype(f32)
        grad_out[rows, :] = (
            pull * query_scale[i : i + 1, :] + anchor_pull[rows, :] * anchor_seed[i : i + 1, :]
        )
    for copy in near + far:
        copy.wait_send()


def pair_grads(slot_query, slot_of, codes, query_inner, query_resid, passage_inner, passage_resid,
               out_weight, gain, bias, proj):
    any_, vmem, smem = pl.ANY, pltpu.VMEM, pltpu.SMEM
    spec = lambda space: pl.BlockSpec(memory_space=space)
    dma = pltpu.SemaphoreType.DMA
    return pl.pallas_call(
        pair_kernel,
        out_shape=(
            jax.ShapeDtypeStruct((ROWS, HID), f32),
            jax.ShapeDtypeStruct((ROWS, DIM), f32),
            jax.ShapeDtypeStruct((ROWS, DIM), f32),
            jax.ShapeDtypeStruct((ROWS, DIM), f32),
            jax.ShapeDtypeStruct((Q_DEV, DIM), f32),
        ),
        in_specs=[spec(smem), spec(smem), spec(vmem)] + [spec(any_)] * 5 + [spec(vmem)] * 3,
        out_specs=(spec(vmem),) * 5,
        scratch_shapes=[
            vmem((ROWS, FFW), bf16),
            vmem((ROWS, HID), bf16),
            vmem((FFW, HID), bf16),
            vmem((Q_DEV, QLEN, DIM), bf16),
            vmem((Q_DEV, PLEN, DIM), bf16),
            vmem((DEVICES, 1, DIM), jnp.int32),
            vmem((8, WIDE), jnp.int32),
            smem((8, WIDE), jnp.int32),
            vmem((SLOTS, QLEN, DIM), bf16),
            vmem((SLOTS + 1, QLEN, DIM), bf16),
            vmem((SORTED * QLEN, DIM), bf16),
            vmem((SORTED * QLEN, DIM), bf16),
            vmem((SORTED + 1, QLEN, DIM), bf16),
            vmem((SORTED + 1, 1, DIM), f32),
            vmem((SLOTS, DIM), f32),
            vmem((SLOTS + 1, 1, DIM), f32),
            vmem((8, DIM), f32),
            vmem((BLOCKS + 1, PLEN, DIM), f32),
            vmem((SLOTS, QLEN, DIM), bf16),
            vmem((SLOTS, QLEN, DIM), bf16),
            vmem((Q_ROWS, DIM), bf16),
            vmem((Q_ROWS, DIM), f32),
            vmem((Q_DEV, DIM), f32),
            vmem((2, Q_DEV, DIM), f32),
            vmem((7, Q_DEV, DIM), f32),
            vmem((15, Q_DEV, DIM), f32),
            dma((5,)), dma, dma, dma, dma, dma, dma, dma, dma((22,)), dma((22,)),
        ],
        compiler_params=pltpu.CompilerParams(
            collective_id=1, has_side_effects=True, vmem_limit_bytes=58 * MIB
        ),
        name="pair_grads",
    )(slot_query, slot_of, codes, query_inner, query_resid, passage_inner, passage_resid, out_weight,
      gain, bias, proj)


def add_rows(out, out_at, terms, rows, chunk):
    def body(i, carry):
        at = pl.multiple_of(i * chunk, chunk)
        total = None
        for ref, start in terms:
            value = ref[pl.ds(pl.multiple_of(start + at, 8), chunk), :].astype(f32)
            total = value if total is None else total + value
        out[pl.ds(pl.multiple_of(out_at + at, 8), chunk), :] = total.astype(out.dtype)
        return carry

    lax.fori_loop(0, rows // chunk, body, 0)


def back_kernel(
    query_inner, passage_inner, normed, unit, scale, grad_unit, gain, bias, proj,
    grad_summed, out_ref, side_out,
    inner, grad, side, proj_sum,
    core_in, held, in1, held1, in2, held2, in3,
    score_in, sheld, sin1, sheld1, sin2, sheld2, sin3,
    load_sem, send_sem, recv_sem,
):
    place = position()
    core = place["core"]
    other = (core + 1) % 2
    loads = [
        pltpu.make_async_copy(query_inner, inner.at[pl.ds(0, Q_ROWS)], load_sem.at[0]),
        pltpu.make_async_copy(passage_inner, inner.at[pl.ds(Q_ROWS, P_ROWS)], load_sem.at[1]),
    ]
    for load in loads:
        load.start()
    barrier = pltpu.get_barrier_semaphore()
    peers = [shifted(place, axis, t) for axis in AXES for t in (1, 2, 3)] + [shifted(place, "core", 1)]
    for peer in peers:
        pl.semaphore_signal(barrier, inc=1, device_id=device_at(peer), device_id_type=MESH)

    proj_sum[...] = jnp.zeros_like(proj_sum)

    def back(i, carry):
        here = pl.ds(pl.multiple_of(i * CHUNK, CHUNK), CHUNK)
        u, g = unit[here, :], grad_unit[here, :]
        reciprocal = scale[here, 0:1]
        length = scale[here, DIM - 1 : DIM]
        grad_projected = ((g - u * jnp.sum(u * g, axis=1, keepdims=True)) / length).astype(bf16)
        n = normed[here, :]
        layer_out = (n * gain[...] + bias[...]).astype(bf16)
        proj_sum[...] += dot(layer_out, grad_projected, (0, 0))
        grad_layer = dot(grad_projected, proj[...], (1, 1))
        norm_sums = (
            carry[0] + jnp.sum(grad_layer * n, axis=0, keepdims=True),
            carry[1] + jnp.sum(grad_layer, axis=0, keepdims=True),
        )
        grad_normed = grad_layer * gain[...]
        grad_summed[here, :] = (
            reciprocal
            * (
                grad_normed
                - jnp.mean(grad_normed, axis=1, keepdims=True)
                - n * jnp.mean(grad_normed * n, axis=1, keepdims=True)
            )
        ).astype(bf16)
        return norm_sums

    zero = jnp.zeros((1, HID), f32)
    norm_sums = lax.fori_loop(0, ROWS // CHUNK, back, (zero, zero))
    side[0] = proj_sum[0:SIDE_ROWS, :]
    side[1] = jnp.zeros((SIDE_ROWS, DIM), f32)
    side[1, 0 : HID - SIDE_ROWS, :] = proj_sum[SIDE_ROWS:HID, :]
    for n in range(2):
        for j in range(HID // DIM):
            row = HID - SIDE_ROWS + n * (HID // DIM) + j
            side[1, row : row + 1, :] = norm_sums[n][:, j * DIM : (j + 1) * DIM]

    copies = {}

    def send(phase, part, step, src, dst, peer):
        copy = pltpu.make_async_remote_copy(
            src_ref=src, dst_ref=dst,
            send_sem=send_sem.at[phase, part, step], recv_sem=recv_sem.at[phase, part, step],
            device_id=device_at(peer), device_id_type=MESH,
        )
        copy.start()
        copies[phase, part, step] = copy

    def bufs(part):
        if part < PARTS:
            return dict(
                src=grad.at[part], core_in=core_in.at[part], held=held.at[part],
                ins=(in1.at[part], in2.at[part], in3.at[part]),
                helds=(held1.at[part], held2.at[part]), out=out_ref.at[part], rows=PART_ROWS,
            )
        return dict(
            src=side, core_in=score_in, held=sheld, ins=(sin1, sin2, sin3),
            helds=(sheld1, sheld2), out=side_out, rows=SIDE_ROWS,
        )

    every = range(PARTS + 1)
    pl.semaphore_wait(barrier, len(peers))
    for load in loads:
        load.wait()

    def weights(half):
        def block(g, carry):
            start = pl.multiple_of(half * (FFW // 2) + g * 512, 512)
            product = dot(inner[:, pl.ds(start, 512)], grad_summed[...], (0, 0)).astype(bf16)
            for part in range(PARTS):
                for h in range(2):
                    column = part * 256 + h * DIM
                    at = pl.multiple_of(h * (FFW // 2) + g * 512, 512)
                    grad[part, half, pl.ds(at, 512), :] = product[:, column : column + DIM]
            return carry

        lax.fori_loop(0, 3, block, 0)

    def send_half(part):
        b = bufs(part)
        send(0, part, 0, b["src"].at[other], b["core_in"], shifted(place, "core", 1))

    send_half(PARTS)
    weights(other)
    for part in range(PARTS):
        send_half(part)
    weights(core)

    for part in every:
        b = bufs(part)
        copies[0, part, 0].wait_recv()
        add_rows(b["held"], 0, [(b["src"].at[core], 0), (b["core_in"], 0)], b["rows"], 128)
        rows = b["rows"] // 4
        axis = ORDERS[part][0]
        for t in (1, 2, 3):
            peer = shifted(place, axis, t)
            at = pl.multiple_of(peer[axis] * rows, rows)
            send(1, part, t - 1, b["held"].at[pl.ds(at, rows)], b["ins"][0].at[t - 1], peer)
    for phase in (1, 2, 3):
        for part in every:
            b = bufs(part)
            rows = b["rows"] // 4**phase
            axis = ORDERS[part][phase - 1]
            here = b["held"] if phase == 1 else b["helds"][phase - 2]
            for t in (1, 2, 3):
                copies[phase, part, t - 1].wait_recv()
            terms = [(here, place[axis] * rows)] + [(b["ins"][phase - 1].at[t], 0) for t in range(3)]
            if phase < 3:
                target, at = b["helds"][phase - 1], 0
            else:
                target = b["out"].at[core]
                at = sum(place[a] * (b["rows"] // 4 ** (n + 1)) for n, a in enumerate(ORDERS[part]))
            add_rows(target, at, terms, rows, 96 if rows % 96 == 0 else min(rows, 64))
            if phase < 3:
                axis = ORDERS[part][phase]
                rows = rows // 4
                for t in (1, 2, 3):
                    peer = shifted(place, axis, t)
                    start = pl.multiple_of(peer[axis] * rows, rows)
                    send(phase + 1, part, t - 1, target.at[pl.ds(start, rows)], b["ins"][phase].at[t - 1], peer)
            else:
                axis = ORDERS[part][2]
                block = target.at[pl.ds(pl.multiple_of(at, 8 if part == PARTS else 16), rows)]
                for t in (1, 2, 3):
                    send(4, part, t - 1, block, block, shifted(place, axis, t))
    for phase in (4, 5, 6):
        for part in every:
            b = bufs(part)
            for t in (1, 2, 3):
                copies[phase, part, t - 1].wait_recv()
            target = b["out"].at[core]
            if phase < 6:
                depth = 6 - phase
                rows = b["rows"] // 4**depth
                axis = ORDERS[part][depth - 1]
                at = sum(
                    place[a] * (b["rows"] // 4 ** (n + 1)) for n, a in enumerate(ORDERS[part][:depth])
                )
                block = target.at[pl.ds(pl.multiple_of(at, 8 if part == PARTS else 16), rows)]
                for t in (1, 2, 3):
                    send(phase + 1, part, t - 1, block, block, shifted(place, axis, t))
            else:
                send(7, part, 0, target, target, shifted(place, "core", 1))
    for part in every:
        copies[7, part, 0].wait_recv()
    for copy in copies.values():
        copy.wait_send()


def back(query_inner, passage_inner, normed, unit, scale, grad_unit, gain, bias, proj):
    spec = lambda space: pl.BlockSpec(memory_space=space)
    vm = lambda *shape: pltpu.VMEM(shape, bf16)
    vf = lambda *shape: pltpu.VMEM(shape, f32)
    r = PART_ROWS
    s = SIDE_ROWS
    return pl.pallas_call(
        back_kernel,
        out_shape=(
            jax.ShapeDtypeStruct((ROWS, HID), bf16),
            jax.ShapeDtypeStruct((PARTS, 2, r, DIM), bf16),
            jax.ShapeDtypeStruct((2, s, DIM), f32),
        ),
        in_specs=[spec(pl.ANY)] * 2 + [spec(pltpu.VMEM)] * 7,
        out_specs=(spec(pltpu.VMEM),) * 3,
        scratch_shapes=[
            vm(ROWS, FFW), vm(PARTS, 2, r, DIM), vf(2, s, DIM), vf(HID, DIM),
            vm(PARTS, r, DIM), vm(PARTS, r, DIM), vm(PARTS, 3, r // 4, DIM), vm(PARTS, r // 4, DIM),
            vm(PARTS, 3, r // 16, DIM), vm(PARTS, r // 16, DIM), vm(PARTS, 3, r // 64, DIM),
            vf(s, DIM), vf(s, DIM), vf(3, s // 4, DIM), vf(s // 4, DIM),
            vf(3, s // 16, DIM), vf(s // 16, DIM), vf(3, s // 64, DIM),
            pltpu.SemaphoreType.DMA((2,)),
            pltpu.SemaphoreType.DMA((8, PARTS + 1, 3)),
            pltpu.SemaphoreType.DMA((8, PARTS + 1, 3)),
        ],
        compiler_params=pltpu.CompilerParams(
            collective_id=3, has_side_effects=True, vmem_limit_bytes=58 * MIB
        ),
        name="back",
    )(query_inner, passage_inner, normed, unit, scale, grad_unit, gain, bias, proj)


def finish_kernel(grad_summed, weight, total, query_inner, passage_inner, query_resid, passage_resid, summed):
    i = pl.program_id(0)
    for part in range(PARTS):
        for h in range(2):
            column = part * 256 + h * DIM
            summed[:, column : column + DIM] = total[part, 0, h, 0].astype(f32)

    def inner_grad(ref):
        def block(n, carry):
            at = pl.ds(pl.multiple_of(n * HID, HID), HID)
            ref[:, at] = dot(grad_summed[...], weight[at, :], (1, 1)).astype(bf16)
            return carry

        lax.fori_loop(0, FFW // HID, block, 0)

    @pl.when(i == 0)
    def _():
        inner_grad(query_inner)
        query_resid[...] = grad_summed[...]

    @pl.when((i > 0) & (i < ROWS // CHUNK))
    def _():
        inner_grad(passage_inner)
        passage_resid[...] = grad_summed[...]


def finish(grad_summed, weight, total):
    steps = 6
    q_at = lambda i: (0, 0)
    p_at = lambda i: (jnp.clip(i - 1, 0, P_ROWS // CHUNK - 1), 0)
    return pl.pallas_call(
        finish_kernel,
        grid=(steps,),
        out_shape=(
            jax.ShapeDtypeStruct((Q_ROWS, FFW), bf16),
            jax.ShapeDtypeStruct((P_ROWS, FFW), bf16),
            jax.ShapeDtypeStruct((Q_ROWS, HID), bf16),
            jax.ShapeDtypeStruct((P_ROWS, HID), bf16),
            jax.ShapeDtypeStruct((FFW, HID), f32),
        ),
        in_specs=[
            pl.BlockSpec((CHUNK, HID), lambda i: (jnp.minimum(i, ROWS // CHUNK - 1), 0)),
            pl.BlockSpec((FFW, HID), lambda i: (0, 0)),
            pl.BlockSpec((PARTS, 1, 2, 1, 512, DIM), lambda i: (0, i // 3, 0, i % 3, 0, 0)),
        ],
        out_specs=(
            pl.BlockSpec((CHUNK, FFW), q_at),
            pl.BlockSpec((CHUNK, FFW), p_at),
            pl.BlockSpec((CHUNK, HID), q_at),
            pl.BlockSpec((CHUNK, HID), p_at),
            pl.BlockSpec((512, HID), lambda i: (i, 0)),
        ),
        compiler_params=pltpu.CompilerParams(vmem_limit_bytes=48 * MIB),
        name="finish",
    )(grad_summed, weight, total)


def ask_slots(negative_owner, negative_index):
    place = position()
    owner = negative_owner.reshape(-1)
    index = negative_index.reshape(-1)
    away = (
        ((owner // 32 + 4 - place["x"]) % 4) * 32
        + (((owner // 8) % 4 + 4 - place["z"]) % 4) * 8
        + (((owner // 4) % 2 + 2 - place["core"]) % 2) * 4
        + (owner % 4 + 4 - place["y"]) % 4
    )
    pair = jnp.arange(Q_DEV * NEG, dtype=jnp.int32)
    rank = jnp.sum(
        ((owner[None, :] == owner[:, None]) & (pair[None, :] < pair[:, None])).astype(jnp.int32), axis=1
    )
    slot_of = away * CAP + rank
    hit = slot_of[None, :] == jnp.arange(SLOTS, dtype=jnp.int32)[:, None]
    slot_query = jnp.sum(jnp.where(hit, pair // NEG, 0), axis=1)
    codes = Q_DEV + jnp.sum(jnp.where(hit, pair // NEG * 16 + index - Q_DEV, 0), axis=1)
    codes = jnp.pad(codes.reshape(DEVICES, 1, CAP), ((0, 0), (0, 0), (0, DIM - CAP)))
    return slot_query, slot_of, codes


def local(
    query_inner,
    query_resid,
    passage_inner,
    passage_resid,
    out_weight,
    norm_gain,
    norm_bias,
    proj_weight,
    negative_owner,
    negative_index,
):
    query_inner = query_inner.reshape(Q_ROWS, FFW)
    passage_inner = passage_inner.reshape(P_ROWS, FFW)
    gain = norm_gain.reshape(1, HID)
    bias = norm_bias.reshape(1, HID)
    slot_query, slot_of, codes = ask_slots(negative_owner, negative_index)
    normed, unit, scale, grad_unit, loss = pair_grads(
        slot_query, slot_of, codes, query_inner, query_resid.reshape(Q_ROWS, HID), passage_inner,
        passage_resid.reshape(P_ROWS, HID), out_weight, gain, bias, proj_weight,
    )
    grad_summed, total, side = back(
        query_inner, passage_inner, normed, unit, scale, grad_unit, gain, bias, proj_weight
    )
    grads = finish(grad_summed, out_weight, total.reshape(PARTS, 2, 2, 3, 512, DIM))
    side = side.reshape(2 * SIDE_ROWS, DIM)
    return (
        loss[:, 0],
        grads[0].reshape(Q_DEV, QLEN, FFW),
        grads[2].reshape(Q_DEV, QLEN, HID),
        grads[1].reshape(Q_DEV, PLEN, FFW),
        grads[3].reshape(Q_DEV, PLEN, HID),
        grads[4],
        side[:HID],
        side[HID : HID + 2 * HID // DIM].reshape(2, HID),
    )


def solution(mesh):
    in_specs = (
        P(("dp", "group"), None, None),
        P(("dp", "group"), None, None),
        P(("dp", "group"), None, None),
        P(("dp", "group"), None, None),
        P(),
        P(),
        P(),
        P(),
        P(("dp", "group"), None),
        P(("dp", "group"), None),
    )
    out_specs = (
        P(("dp", "group")),
        P(("dp", "group"), None, None),
        P(("dp", "group"), None, None),
        P(("dp", "group"), None, None),
        P(("dp", "group"), None, None),
        P(),
        P(),
        P(),
    )
    return jax.shard_map(local, mesh=mesh, in_specs=in_specs, out_specs=out_specs, check_vma=False)
```

time: 498 us -> 203 us (0.41); the launches traced: 489 us -> 202 us
  waiting for transfers between devices: 178 us -> 0 us
  Pallas kernels: 52.8 us -> 190 us
  local copies, waits for them, and re-layouts: 140 us -> 10.8 us
  matrix products: 63.3 us -> 0 us
  starting transfers between devices: 29.4 us -> 0 us
  other arithmetic: 24.3 us -> 0.94 us
    all_to_all x3 -> x0, waiting for transfers between devices: 178 us -> none  [the longest x1 90.9 us: local(): lax.all_to_all(passage_emb[served], ('dp', 'group'), split_axis=0, concat...]
    pallas_call x1 -> x3, Pallas kernels: 52.8 us -> 190 us  [the longest x1 107 us: pair_grads(): pl.pallas_call(pair_kernel, out_shape=(jax.ShapeDtypeStruct((ROWS, HID),...]
    dot_general x19 -> x0, matrix products: 63.3 us -> none  [the longest x2 15 us: encode_back(): jnp.dot(hidden_in.T, grad_summed, preferred_element_type=jnp.float32)]
    reshape x5, local copies, waits for them, and re-layouts: 38.5 us -> 4.67 us  [the longest x1 1.27 us: local(): gain = norm_gain.reshape(1, HID)]
    convert_element_type x2 -> x0, local copies, waits for them, and re-layouts: 33.6 us -> none  [summed_grads(): total = grad.reshape(PARTS, 2, 2, FFW // 2, DIM).transpose(1, 3, 0, 2, 4)...]
    all_to_all x3 -> x0, starting transfers between devices: 29.4 us -> none  [the longest x1 11.5 us: local(): lax.all_to_all(wanted, ('dp', 'group'), split_axis=0, concat_axis=0, tile...]
    scatter x2 -> x0, local copies, waits for them, and re-layouts: 24.7 us -> none  [the longest x1 23.7 us: local(): outgoing = jnp.zeros((slot_total, PLEN, DIM), jnp.float32).at[pair_slot]....]
    convert_element_type x12 -> x0, other arithmetic: 15.9 us -> none  [the longest x1 9.17 us: local(): outgoing.astype(jnp.bfloat16)]
  transfers between devices with their start and end apart: 3 -> 0, of which waited for: 2 -> 0; matrix products, arithmetic and copies ran while one was open for 8% -> 0% of each run, Pallas kernels for 0% -> 0%
where the time goes in v2:
time: 203 us; the launch traced here: 202 us
  Pallas kernels  190 us (94%)
  local copies, waits for them, and re-layouts  10.8 us (5%)
    pallas_call x1, Pallas kernels, pair_grads(): pl.pallas_call(pair_kernel, out_shape=(jax.ShapeDtypeStruct((ROWS, HID),...  107 us
    pallas_call x1, Pallas kernels, back(): pl.pallas_call(back_kernel, out_shape=(jax.ShapeDtypeStruct((ROWS, HID),...  66.3 us
    pallas_call x1, Pallas kernels, finish(): pl.pallas_call(finish_kernel, grid=(steps,), out_shape=(jax.ShapeDtypeStr...  16.6 us

profile of v2, /device:TPU:1, one launch (start us, length us, event | category | flops | bytes accessed | tf_op | source)
XLA Modules:
  0.0 202.3 jit_solution(5642100430050190888)
XLA Ops:
  0.7 0.8 reshape.228
  1.4 0.2 convert_reduce_fusion
  1.7 0.0 copy-start.1
  1.7 0.8 reshape.229
  2.5 0.7 select_reduce_fusion
  3.2 1.3 reshape.234.gain
  4.4 1.3 reshape.235.bias
  5.7 0.1 add.177
  5.8 0.7 pad.4.codes
  6.5 0.0 copy-done.1
  6.5 107.0 %pair_grads.1 = (f32[1280,768]{1,0:T(8,128)}, f32[1280,128]{1,0:T(8,128)}, f32[1280,128]{1,0:T(8,128)}, f32[1280,128]{1,0:T(8,128)}, f32[8,128]{1,0:T(8,128)}) custom-call(s32[256]{0:T(256)} %get-tuple-element.35.slot_query, s32[128]{0:T(128)} %copy-done.1, s32[128,1,128]{2,1,0:T(1,128)} %pad.4.codes, bf16[256,3072]{1,0:T(8,128)(2,1)} %bitcast.13, ...), custom_call_target="tpu_custom_call" | custom-call | tf_op jit(solution)/shard_map/pair_grads/pallas_call | solution.py:396
  113.5 1.3 slice_reduce_fusion
  114.8 66.3 %back.1 = (bf16[1280,768]{1,0:T(8,128)(2,1)}, bf16[3,2,3072,128]{3,2,1,0:T(8,128)(2,1)}, f32[2,512,128]{2,1,0:T(8,128)}) custom-call(bf16[256,3072]{1,0:T(8,128)(2,1)} %bitcast.14, bf16[1024,3072]{1,0:T(8,128)(2,1)} %bitcast.12, f32[1280,768]{1,0:T(8,128)} %get-tuple-element.22.normed, f32[1280,128]{1,0:T(8,128)} %get-tuple-element.23.unit, ...), custom_call_target="tpu_custom_call" | custom-call | tf_op jit(solution)/shard_map/back/pallas_call | solution.py:634
  181.1 0.7 slice.13
  181.8 1.8 slice.12
  183.6 0.6 reshape.242
  184.2 0.0 copy-start
  184.2 1.5 copy-done
  185.7 16.6 %finish.1 = (bf16[256,3072]{1,0:T(8,128)(2,1)}, bf16[1024,3072]{1,0:T(8,128)(2,1)}, bf16[256,768]{1,0:T(8,128)(2,1)}, bf16[1024,768]{1,0:T(8,128)(2,1)}, f32[3072,768]{1,0:T(8,128)}) custom-call(bf16[1280,768]{1,0:T(8,128)(2,1)S(1)} %copy-done, bf16[3072,768]{1,0:T(8,128)(2,1)} %weight.1, bf16[3,2,2,3,512,128]{5,4,3,2,1,0:T(8,128)(2,1)} %bitcast.15), custom_call_target="tpu_custom_call" | custom-call | tf_op jit(solution)/shard_map/finish/pallas_call | solution.py:690
  (3 shorter events, 0.0 us)
Async XLA Ops:
  1.7 4.9 %copy-start.1 = (s32[128]{0:T(128)}, s32[128]{0:T(128)S(1)}, u32[]{:S(2)}) copy-start(s32[128]{0:T(128)S(1)} %multiply_add_fusion.slot_of) | copy-start | bytes 1540
  184.2 1.5 copy-start

commit v3 on v2

--- a/solution.py
+++ b/solution.py
@@ -24,6 +24,8 @@
 BLOCKS = SLOTS // 8 + Q_DEV
 SORTED = BLOCKS * 8
 WIDE = 384
+SPREAD = 37
+SCORE_STEP = 4
 
 MESH = pl.DeviceIdType.MESH
 MIB = 1024 * 1024
@@ -118,17 +120,37 @@
     return weights, pool_temp * jnp.sum(logs, axis=1)
 
 
-def pair_kernel(
+def add_rows(out, out_at, terms, rows, chunk):
+    def body(i, carry):
+        at = pl.multiple_of(i * chunk, chunk)
+        total = None
+        for ref, start in terms:
+            value = ref[pl.ds(pl.multiple_of(start + at, 8), chunk), :].astype(f32)
+            total = value if total is None else total + value
+        out[pl.ds(pl.multiple_of(out_at + at, 8), chunk), :] = total.astype(out.dtype)
+        return carry
+
+    lax.fori_loop(0, rows // chunk, body, 0)
+
+
+def step_kernel(
     slot_query, slot_of, codes,
-    query_inner, query_resid, passage_inner, passage_resid, out_weight, gain, bias, proj,
-    normed_out, unit_out, scale_out, grad_out, loss_out,
-    inner, resid, weight, query_emb, passage_emb, codes_in, table, table_s,
+    query_inner, query_resid, passage_inner, passage_resid, out_weight, gain_in, bias_in, proj,
+    grad_summed, out_ref, side_out, loss_out,
+    gain, bias, inner, resid, weight, normed_out, unit_out, scale_out, grad_out,
+    query_emb, passage_emb, codes_in, table, table_s,
     asks_out, asks_in, sorted_q, sorted_w, sorted_pull, sorted_exp, slot_exp, slot_seed, block_seed, chain,
     pulls_out, pulls_in, anchor_w, anchor_pull, anchor_score,
     sums, sums_in1, sums_in2,
+    grad, side, proj_sum,
+    core_in, held, in1, held1, in2, held2, in3,
+    score_in, sheld, sin1, sheld1, sin2, sheld2, sin3,
     load_sem, table_sem, code_send, code_recv, ask_send, ask_recv, pull_send, pull_recv, sum_send, sum_recv,
+    send_sem, recv_sem,
 ):
     place = position()
+    core = place["core"]
+    other = (core + 1) % 2
     me = number_of(place)
     lane_row = iota((1, DIM), 1)
 
@@ -155,6 +177,9 @@
     slot_seed[SLOTS] = jnp.zeros((1, DIM), f32)
     chain[BLOCKS] = jnp.zeros((PLEN, DIM), f32)
     codes_in[0] = codes[0]
+    gain[...] = gain_in[...].reshape(1, HID)
+    bias[...] = bias_in[...].reshape(1, HID)
+    proj_sum[...] = jnp.zeros_like(proj_sum)
     pl.semaphore_wait(barrier, DEVICES - 1)
 
     def code_copy(t):
@@ -202,7 +227,8 @@
     for r in range(CAP):
         asks_in[r] = take_query(r)
 
-    def send_ask(t, carry):
+    def send_ask(i, carry):
+        t = (i * SPREAD) % DEVICES
         for r in range(CAP):
             asks_out[t * CAP + r] = take_query(t * CAP + r)
         ask_copy(t).start()
@@ -253,21 +279,24 @@
     )
     all_asks.wait()
 
-    def score_block(b, carry):
-        at = pl.multiple_of(b * CHUNK, CHUNK)
-        for k in range(8):
-            asking = asks_in[table_s[0, b * 8 + k]]
-            sorted_q[pl.ds(pl.multiple_of(at + k * QLEN, QLEN), QLEN), :] = asking
-        passage = passage_emb[table_s[3, b]]
-        weights, score = pool(sorted_q[pl.ds(at, CHUNK), :], passage)
-        sorted_w[pl.ds(at, CHUNK), :] = weights
-        exp_score = jnp.exp(score)
-        sorted_exp[pl.ds(b * 8, 8)] = exp_score.reshape(8, 1, DIM)
-        pull = dot(weights, passage, (1, 0)).reshape(8, QLEN, DIM) * exp_score.reshape(8, 1, DIM)
-        sorted_pull[pl.ds(b * 8, 8)] = pull.astype(bf16)
-        return carry
-
-    lax.fori_loop(0, BLOCKS, score_block, 0)
+    def score_blocks(n, carry):
+        blocks = [n * SCORE_STEP + m for m in range(SCORE_STEP)]
+        ats = [pl.multiple_of(b * CHUNK, CHUNK) for b in blocks]
+        for b, at in zip(blocks, ats):
+            for k in range(8):
+                asking = asks_in[table_s[0, b * 8 + k]]
+                sorted_q[pl.ds(pl.multiple_of(at + k * QLEN, QLEN), QLEN), :] = asking
+        passages = [passage_emb[table_s[3, b]] for b in blocks]
+        pooled = [pool(sorted_q[pl.ds(at, CHUNK), :], p) for at, p in zip(ats, passages)]
+        pulls = [dot(weights, p, (1, 0)).reshape(8, QLEN, DIM) for (weights, _), p in zip(pooled, passages)]
+        for b, at, (weights, score), pull in zip(blocks, ats, pooled, pulls):
+            sorted_w[pl.ds(at, CHUNK), :] = weights
+            exp_score = jnp.exp(score).reshape(8, 1, DIM)
+            sorted_exp[pl.ds(b * 8, 8)] = exp_score
+            sorted_pull[pl.ds(b * 8, 8)] = (pull * exp_score).astype(bf16)
+        return carry
+
+    lax.fori_loop(0, BLOCKS // SCORE_STEP, score_blocks, 0)
 
     def exp_of(t, carry):
         for r in range(CAP):
@@ -329,7 +358,8 @@
     for r in range(CAP):
         pulls_in[r] = take_pull(r)
 
-    def send_pull(t, carry):
+    def send_pull(i, carry):
+        t = (i * SPREAD) % DEVICES
         for r in range(CAP):
             pulls_out[t * CAP + r] = take_pull(t * CAP + r)
         pull_copy(t).start()
@@ -371,120 +401,13 @@
         push += chain[table_s[5, p]]
         grad_out[pl.ds(Q_ROWS + p * PLEN, PLEN), :] = push
 
-    pltpu.make_async_remote_copy(
-        src_ref=asked(pulls_out), dst_ref=asked(pulls_in), send_sem=pull_send, recv_sem=pull_recv,
-        device_id=device_at(offset(place, 1, 1)), device_id_type=MESH,
-    ).wait()
-    query_scale = loss_scale / own_total
-    for i in range(Q_DEV):
-        rows = pl.ds(i * QLEN, QLEN)
-        pull = jnp.zeros((QLEN, DIM), f32)
-        for k in range(NEG):
-            pull += pulls_in[slot_of[i * NEG + k]].astype(f32)
-        grad_out[rows, :] = (
-            pull * query_scale[i : i + 1, :] + anchor_pull[rows, :] * anchor_seed[i : i + 1, :]
-        )
-    for copy in near + far:
-        copy.wait_send()
-
-
-def pair_grads(slot_query, slot_of, codes, query_inner, query_resid, passage_inner, passage_resid,
-               out_weight, gain, bias, proj):
-    any_, vmem, smem = pl.ANY, pltpu.VMEM, pltpu.SMEM
-    spec = lambda space: pl.BlockSpec(memory_space=space)
-    dma = pltpu.SemaphoreType.DMA
-    return pl.pallas_call(
-        pair_kernel,
-        out_shape=(
-            jax.ShapeDtypeStruct((ROWS, HID), f32),
-            jax.ShapeDtypeStruct((ROWS, DIM), f32),
-            jax.ShapeDtypeStruct((ROWS, DIM), f32),
-            jax.ShapeDtypeStruct((ROWS, DIM), f32),
-            jax.ShapeDtypeStruct((Q_DEV, DIM), f32),
-        ),
-        in_specs=[spec(smem), spec(smem), spec(vmem)] + [spec(any_)] * 5 + [spec(vmem)] * 3,
-        out_specs=(spec(vmem),) * 5,
-        scratch_shapes=[
-            vmem((ROWS, FFW), bf16),
-            vmem((ROWS, HID), bf16),
-            vmem((FFW, HID), bf16),
-            vmem((Q_DEV, QLEN, DIM), bf16),
-            vmem((Q_DEV, PLEN, DIM), bf16),
-            vmem((DEVICES, 1, DIM), jnp.int32),
-            vmem((8, WIDE), jnp.int32),
-            smem((8, WIDE), jnp.int32),
-            vmem((SLOTS, QLEN, DIM), bf16),
-            vmem((SLOTS + 1, QLEN, DIM), bf16),
-            vmem((SORTED * QLEN, DIM), bf16),
-            vmem((SORTED * QLEN, DIM), bf16),
-            vmem((SORTED + 1, QLEN, DIM), bf16),
-            vmem((SORTED + 1, 1, DIM), f32),
-            vmem((SLOTS, DIM), f32),
-            vmem((SLOTS + 1, 1, DIM), f32),
-            vmem((8, DIM), f32),
-            vmem((BLOCKS + 1, PLEN, DIM), f32),
-            vmem((SLOTS, QLEN, DIM), bf16),
-            vmem((SLOTS, QLEN, DIM), bf16),
-            vmem((Q_ROWS, DIM), bf16),
-            vmem((Q_ROWS, DIM), f32),
-            vmem((Q_DEV, DIM), f32),
-            vmem((2, Q_DEV, DIM), f32),
-            vmem((7, Q_DEV, DIM), f32),
-            vmem((15, Q_DEV, DIM), f32),
-            dma((5,)), dma, dma, dma, dma, dma, dma, dma, dma((22,)), dma((22,)),
-        ],
-        compiler_params=pltpu.CompilerParams(
-            collective_id=1, has_side_effects=True, vmem_limit_bytes=58 * MIB
-        ),
-        name="pair_grads",
-    )(slot_query, slot_of, codes, query_inner, query_resid, passage_inner, passage_resid, out_weight,
-      gain, bias, proj)
-
-
-def add_rows(out, out_at, terms, rows, chunk):
-    def body(i, carry):
-        at = pl.multiple_of(i * chunk, chunk)
-        total = None
-        for ref, start in terms:
-            value = ref[pl.ds(pl.multiple_of(start + at, 8), chunk), :].astype(f32)
-            total = value if total is None else total + value
-        out[pl.ds(pl.multiple_of(out_at + at, 8), chunk), :] = total.astype(out.dtype)
-        return carry
-
-    lax.fori_loop(0, rows // chunk, body, 0)
-
-
-def back_kernel(
-    query_inner, passage_inner, normed, unit, scale, grad_unit, gain, bias, proj,
-    grad_summed, out_ref, side_out,
-    inner, grad, side, proj_sum,
-    core_in, held, in1, held1, in2, held2, in3,
-    score_in, sheld, sin1, sheld1, sin2, sheld2, sin3,
-    load_sem, send_sem, recv_sem,
-):
-    place = position()
-    core = place["core"]
-    other = (core + 1) % 2
-    loads = [
-        pltpu.make_async_copy(query_inner, inner.at[pl.ds(0, Q_ROWS)], load_sem.at[0]),
-        pltpu.make_async_copy(passage_inner, inner.at[pl.ds(Q_ROWS, P_ROWS)], load_sem.at[1]),
-    ]
-    for load in loads:
-        load.start()
-    barrier = pltpu.get_barrier_semaphore()
-    peers = [shifted(place, axis, t) for axis in AXES for t in (1, 2, 3)] + [shifted(place, "core", 1)]
-    for peer in peers:
-        pl.semaphore_signal(barrier, inc=1, device_id=device_at(peer), device_id_type=MESH)
-
-    proj_sum[...] = jnp.zeros_like(proj_sum)
-
     def back(i, carry):
-        here = pl.ds(pl.multiple_of(i * CHUNK, CHUNK), CHUNK)
-        u, g = unit[here, :], grad_unit[here, :]
-        reciprocal = scale[here, 0:1]
-        length = scale[here, DIM - 1 : DIM]
+        here = pl.ds(i * CHUNK if isinstance(i, int) else pl.multiple_of(i * CHUNK, CHUNK), CHUNK)
+        u, g = unit_out[here, :], grad_out[here, :]
+        reciprocal = scale_out[here, 0:1]
+        length = scale_out[here, DIM - 1 : DIM]
         grad_projected = ((g - u * jnp.sum(u * g, axis=1, keepdims=True)) / length).astype(bf16)
-        n = normed[here, :]
+        n = normed_out[here, :]
         layer_out = (n * gain[...] + bias[...]).astype(bf16)
         proj_sum[...] += dot(layer_out, grad_projected, (0, 0))
         grad_layer = dot(grad_projected, proj[...], (1, 1))
@@ -503,8 +426,42 @@
         ).astype(bf16)
         return norm_sums
 
+    def weights(half, first, count, more):
+        def block(g, carry):
+            start = pl.multiple_of(half * (FFW // 2) + g * 512, 512)
+            tokens = pl.ds(first, count)
+            product = dot(inner[tokens, pl.ds(start, 512)], grad_summed[tokens, :], (0, 0))
+            for part in range(PARTS):
+                for h in range(2):
+                    column = part * 256 + h * DIM
+                    at = pl.ds(pl.multiple_of(h * (FFW // 2) + g * 512, 512), 512)
+                    value = product[:, column : column + DIM]
+                    if more:
+                        value += grad[part, half, at, :].astype(f32)
+                    grad[part, half, at, :] = value.astype(bf16)
+            return carry
+
+        lax.fori_loop(0, 3, block, 0)
+
     zero = jnp.zeros((1, HID), f32)
-    norm_sums = lax.fori_loop(0, ROWS // CHUNK, back, (zero, zero))
+    norm_sums = lax.fori_loop(1, ROWS // CHUNK, back, (zero, zero))
+    for half in range(2):
+        weights(half, Q_ROWS, P_ROWS, False)
+
+    pltpu.make_async_remote_copy(
+        src_ref=asked(pulls_out), dst_ref=asked(pulls_in), send_sem=pull_send, recv_sem=pull_recv,
+        device_id=device_at(offset(place, 1, 1)), device_id_type=MESH,
+    ).wait()
+    query_scale = loss_scale / own_total
+    for i in range(Q_DEV):
+        rows = pl.ds(i * QLEN, QLEN)
+        pull = jnp.zeros((QLEN, DIM), f32)
+        for k in range(NEG):
+            pull += pulls_in[slot_of[i, k]].astype(f32)
+        grad_out[rows, :] = (
+            pull * query_scale[i : i + 1, :] + anchor_pull[rows, :] * anchor_seed[i : i + 1, :]
+        )
+    norm_sums = back(0, norm_sums)
     side[0] = proj_sum[0:SIDE_ROWS, :]
     side[1] = jnp.zeros((SIDE_ROWS, DIM), f32)
     side[1, 0 : HID - SIDE_ROWS, :] = proj_sum[SIDE_ROWS:HID, :]
@@ -537,32 +494,16 @@
         )
 
     every = range(PARTS + 1)
-    pl.semaphore_wait(barrier, len(peers))
-    for load in loads:
-        load.wait()
-
-    def weights(half):
-        def block(g, carry):
-            start = pl.multiple_of(half * (FFW // 2) + g * 512, 512)
-            product = dot(inner[:, pl.ds(start, 512)], grad_summed[...], (0, 0)).astype(bf16)
-            for part in range(PARTS):
-                for h in range(2):
-                    column = part * 256 + h * DIM
-                    at = pl.multiple_of(h * (FFW // 2) + g * 512, 512)
-                    grad[part, half, pl.ds(at, 512), :] = product[:, column : column + DIM]
-            return carry
-
-        lax.fori_loop(0, 3, block, 0)
 
     def send_half(part):
         b = bufs(part)
         send(0, part, 0, b["src"].at[other], b["core_in"], shifted(place, "core", 1))
 
     send_half(PARTS)
-    weights(other)
+    weights(other, 0, Q_ROWS, True)
     for part in range(PARTS):
         send_half(part)
-    weights(core)
+    weights(core, 0, Q_ROWS, True)
 
     for part in every:
         b = bufs(part)
@@ -623,115 +564,145 @@
         copies[7, part, 0].wait_recv()
     for copy in copies.values():
         copy.wait_send()
-
-
-def back(query_inner, passage_inner, normed, unit, scale, grad_unit, gain, bias, proj):
+    for copy in near + far:
+        copy.wait_send()
+
+
+def step(slot_query, slot_of, codes, query_inner, query_resid, passage_inner, passage_resid,
+         out_weight, gain, bias, proj):
+    any_, vmem, smem = pl.ANY, pltpu.VMEM, pltpu.SMEM
     spec = lambda space: pl.BlockSpec(memory_space=space)
-    vm = lambda *shape: pltpu.VMEM(shape, bf16)
-    vf = lambda *shape: pltpu.VMEM(shape, f32)
+    dma = pltpu.SemaphoreType.DMA
+    vm = lambda *shape: vmem(shape, bf16)
+    vf = lambda *shape: vmem(shape, f32)
     r = PART_ROWS
     s = SIDE_ROWS
     return pl.pallas_call(
-        back_kernel,
+        step_kernel,
         out_shape=(
             jax.ShapeDtypeStruct((ROWS, HID), bf16),
             jax.ShapeDtypeStruct((PARTS, 2, r, DIM), bf16),
             jax.ShapeDtypeStruct((2, s, DIM), f32),
+            jax.ShapeDtypeStruct((Q_DEV, DIM), f32),
         ),
-        in_specs=[spec(pl.ANY)] * 2 + [spec(pltpu.VMEM)] * 7,
-        out_specs=(spec(pltpu.VMEM),) * 3,
+        in_specs=[spec(smem), spec(smem), spec(vmem)] + [spec(any_)] * 5 + [spec(vmem)] * 3,
+        out_specs=(spec(vmem),) * 4,
         scratch_shapes=[
-            vm(ROWS, FFW), vm(PARTS, 2, r, DIM), vf(2, s, DIM), vf(HID, DIM),
+            vf(1, HID), vf(1, HID),
+            vm(ROWS, FFW), vm(ROWS, HID), vm(FFW, HID),
+            vf(ROWS, HID), vf(ROWS, DIM), vf(ROWS, DIM), vf(ROWS, DIM),
+            vm(Q_DEV, QLEN, DIM), vm(Q_DEV, PLEN, DIM),
+            vmem((DEVICES, 1, DIM), jnp.int32), vmem((8, WIDE), jnp.int32), smem((8, WIDE), jnp.int32),
+            vm(SLOTS, QLEN, DIM), vm(SLOTS + 1, QLEN, DIM),
+            vm(SORTED * QLEN, DIM), vm(SORTED * QLEN, DIM), vm(SORTED + 1, QLEN, DIM),
+            vf(SORTED + 1, 1, DIM), vf(SLOTS, DIM), vf(SLOTS + 1, 1, DIM), vf(8, DIM),
+            vf(BLOCKS + 1, PLEN, DIM),
+            vm(SLOTS, QLEN, DIM), vm(SLOTS, QLEN, DIM),
+            vm(Q_ROWS, DIM), vf(Q_ROWS, DIM), vf(Q_DEV, DIM),
+            vf(2, Q_DEV, DIM), vf(7, Q_DEV, DIM), vf(15, Q_DEV, DIM),
+            vm(PARTS, 2, r, DIM), vf(2, s, DIM), vf(HID, DIM),
             vm(PARTS, r, DIM), vm(PARTS, r, DIM), vm(PARTS, 3, r // 4, DIM), vm(PARTS, r // 4, DIM),
             vm(PARTS, 3, r // 16, DIM), vm(PARTS, r // 16, DIM), vm(PARTS, 3, r // 64, DIM),
             vf(s, DIM), vf(s, DIM), vf(3, s // 4, DIM), vf(s // 4, DIM),
             vf(3, s // 16, DIM), vf(s // 16, DIM), vf(3, s // 64, DIM),
-            pltpu.SemaphoreType.DMA((2,)),
-            pltpu.SemaphoreType.DMA((8, PARTS + 1, 3)),
-            pltpu.SemaphoreType.DMA((8, PARTS + 1, 3)),
+            dma((5,)), dma, dma, dma, dma, dma, dma, dma, dma((22,)), dma((22,)),
+            dma((8, PARTS + 1, 3)), dma((8, PARTS + 1, 3)),
         ],
         compiler_params=pltpu.CompilerParams(
-            collective_id=3, has_side_effects=True, vmem_limit_bytes=58 * MIB
+            collective_id=1, has_side_effects=True, vmem_limit_bytes=63 * MIB
         ),
-        name="back",
-    )(query_inner, passage_inner, normed, unit, scale, grad_unit, gain, bias, proj)
-
-
-def finish_kernel(grad_summed, weight, total, query_inner, passage_inner, query_resid, passage_resid, summed):
-    i = pl.program_id(0)
+        name="step",
+    )(slot_query, slot_of, codes, query_inner, query_resid, passage_inner, passage_resid, out_weight,
+      gain, bias, proj)
+
+
+def finish_kernel(
+    grad_summed, weight, total, side, loss,
+    query_inner, passage_inner, query_resid, passage_resid, summed, proj_grad, norm_grad, query_loss,
+):
     for part in range(PARTS):
         for h in range(2):
             column = part * 256 + h * DIM
             summed[:, column : column + DIM] = total[part, 0, h, 0].astype(f32)
-
-    def inner_grad(ref):
-        def block(n, carry):
-            at = pl.ds(pl.multiple_of(n * HID, HID), HID)
-            ref[:, at] = dot(grad_summed[...], weight[at, :], (1, 1)).astype(bf16)
-            return carry
-
-        lax.fori_loop(0, FFW // HID, block, 0)
-
-    @pl.when(i == 0)
+    query_inner[...] = dot(grad_summed[0:Q_ROWS, :], weight[...], (1, 1)).astype(bf16)
+
+    def block(n, carry):
+        rows = pl.ds(pl.multiple_of(n * CHUNK, CHUNK), CHUNK)
+        from_rows = pl.ds(pl.multiple_of(Q_ROWS + n * CHUNK, CHUNK), CHUNK)
+        passage_inner[rows, :] = dot(grad_summed[from_rows, :], weight[...], (1, 1)).astype(bf16)
+        return carry
+
+    lax.fori_loop(0, P_ROWS // CHUNK, block, 0)
+
+    @pl.when(pl.program_id(0) == 0)
     def _():
-        inner_grad(query_inner)
-        query_resid[...] = grad_summed[...]
-
-    @pl.when((i > 0) & (i < ROWS // CHUNK))
-    def _():
-        inner_grad(passage_inner)
-        passage_resid[...] = grad_summed[...]
-
-
-def finish(grad_summed, weight, total):
-    steps = 6
-    q_at = lambda i: (0, 0)
-    p_at = lambda i: (jnp.clip(i - 1, 0, P_ROWS // CHUNK - 1), 0)
+        query_resid[...] = grad_summed[0:Q_ROWS, :]
+        passage_resid[...] = grad_summed[Q_ROWS:ROWS, :]
+        proj_grad[0:SIDE_ROWS, :] = side[0]
+        proj_grad[SIDE_ROWS:HID, :] = side[1, 0 : HID - SIDE_ROWS, :]
+        for n in range(2):
+            for j in range(HID // DIM):
+                row = HID - SIDE_ROWS + n * (HID // DIM) + j
+                norm_grad[n : n + 1, j * DIM : (j + 1) * DIM] = side[1, row : row + 1, :]
+        for i in range(Q_DEV):
+            query_loss[i] = loss[i, 0]
+
+
+def finish(grad_summed, weight, total, side, loss):
+    wide = 512
+    whole = lambda *shape: pl.BlockSpec(shape, lambda i: (0,) * len(shape))
     return pl.pallas_call(
         finish_kernel,
-        grid=(steps,),
+        grid=(FFW // wide,),
         out_shape=(
             jax.ShapeDtypeStruct((Q_ROWS, FFW), bf16),
             jax.ShapeDtypeStruct((P_ROWS, FFW), bf16),
             jax.ShapeDtypeStruct((Q_ROWS, HID), bf16),
             jax.ShapeDtypeStruct((P_ROWS, HID), bf16),
             jax.ShapeDtypeStruct((FFW, HID), f32),
+            jax.ShapeDtypeStruct((HID, DIM), f32),
+            jax.ShapeDtypeStruct((2, HID), f32),
+            jax.ShapeDtypeStruct((Q_DEV,), f32),
         ),
         in_specs=[
-            pl.BlockSpec((CHUNK, HID), lambda i: (jnp.minimum(i, ROWS // CHUNK - 1), 0)),
-            pl.BlockSpec((FFW, HID), lambda i: (0, 0)),
-            pl.BlockSpec((PARTS, 1, 2, 1, 512, DIM), lambda i: (0, i // 3, 0, i % 3, 0, 0)),
+            whole(ROWS, HID),
+            pl.BlockSpec((wide, HID), lambda i: (i, 0)),
+            pl.BlockSpec((PARTS, 1, 2, 1, wide, DIM), lambda i: (0, i // 3, 0, i % 3, 0, 0)),
+            whole(2, SIDE_ROWS, DIM),
+            pl.BlockSpec(memory_space=pltpu.SMEM),
         ],
         out_specs=(
-            pl.BlockSpec((CHUNK, FFW), q_at),
-            pl.BlockSpec((CHUNK, FFW), p_at),
-            pl.BlockSpec((CHUNK, HID), q_at),
-            pl.BlockSpec((CHUNK, HID), p_at),
-            pl.BlockSpec((512, HID), lambda i: (i, 0)),
+            pl.BlockSpec((Q_ROWS, wide), lambda i: (0, i)),
+            pl.BlockSpec((P_ROWS, wide), lambda i: (0, i)),
+            whole(Q_ROWS, HID),
+            whole(P_ROWS, HID),
+            pl.BlockSpec((wide, HID), lambda i: (i, 0)),
+            whole(HID, DIM),
+            whole(2, HID),
+            pl.BlockSpec(memory_space=pltpu.SMEM),
         ),
         compiler_params=pltpu.CompilerParams(vmem_limit_bytes=48 * MIB),
         name="finish",
-    )(grad_summed, weight, total)
+    )(grad_summed, weight, total, side, loss)
 
 
 def ask_slots(negative_owner, negative_index):
     place = position()
-    owner = negative_owner.reshape(-1)
-    index = negative_index.reshape(-1)
+    owner = negative_owner
     away = (
         ((owner // 32 + 4 - place["x"]) % 4) * 32
         + (((owner // 8) % 4 + 4 - place["z"]) % 4) * 8
         + (((owner // 4) % 2 + 2 - place["core"]) % 2) * 4
         + (owner % 4 + 4 - place["y"]) % 4
     )
-    pair = jnp.arange(Q_DEV * NEG, dtype=jnp.int32)
-    rank = jnp.sum(
-        ((owner[None, :] == owner[:, None]) & (pair[None, :] < pair[:, None])).astype(jnp.int32), axis=1
-    )
+    query = jnp.arange(Q_DEV, dtype=jnp.int32)
+    same = owner[None, None] == owner[:, :, None, None]
+    earlier = query[None, None, :, None] < query[:, None, None, None]
+    rank = jnp.sum((same & earlier).astype(jnp.int32), axis=(2, 3))
     slot_of = away * CAP + rank
-    hit = slot_of[None, :] == jnp.arange(SLOTS, dtype=jnp.int32)[:, None]
-    slot_query = jnp.sum(jnp.where(hit, pair // NEG, 0), axis=1)
-    codes = Q_DEV + jnp.sum(jnp.where(hit, pair // NEG * 16 + index - Q_DEV, 0), axis=1)
+    hit = slot_of[None] == jnp.arange(SLOTS, dtype=jnp.int32)[:, None, None]
+    slot_query = jnp.sum(jnp.where(hit, query[:, None], 0), axis=(1, 2))
+    codes = Q_DEV + jnp.sum(jnp.where(hit, query[:, None] * 16 + negative_index - Q_DEV, 0), axis=(1, 2))
     codes = jnp.pad(codes.reshape(DEVICES, 1, CAP), ((0, 0), (0, 0), (0, DIM - CAP)))
     return slot_query, slot_of, codes
 
@@ -750,27 +721,21 @@
 ):
     query_inner = query_inner.reshape(Q_ROWS, FFW)
     passage_inner = passage_inner.reshape(P_ROWS, FFW)
-    gain = norm_gain.reshape(1, HID)
-    bias = norm_bias.reshape(1, HID)
     slot_query, slot_of, codes = ask_slots(negative_owner, negative_index)
-    normed, unit, scale, grad_unit, loss = pair_grads(
+    grad_summed, total, side, loss = step(
         slot_query, slot_of, codes, query_inner, query_resid.reshape(Q_ROWS, HID), passage_inner,
-        passage_resid.reshape(P_ROWS, HID), out_weight, gain, bias, proj_weight,
+        passage_resid.reshape(P_ROWS, HID), out_weight, norm_gain, norm_bias, proj_weight,
     )
-    grad_summed, total, side = back(
-        query_inner, passage_inner, normed, unit, scale, grad_unit, gain, bias, proj_weight
-    )
-    grads = finish(grad_summed, out_weight, total.reshape(PARTS, 2, 2, 3, 512, DIM))
-    side = side.reshape(2 * SIDE_ROWS, DIM)
+    grads = finish(grad_summed, out_weight, total.reshape(PARTS, 2, 2, 3, 512, DIM), side, loss)
     return (
-        loss[:, 0],
+        grads[7],
         grads[0].reshape(Q_DEV, QLEN, FFW),
         grads[2].reshape(Q_DEV, QLEN, HID),
         grads[1].reshape(Q_DEV, PLEN, FFW),
         grads[3].reshape(Q_DEV, PLEN, HID),
         grads[4],
-        side[:HID],
-        side[HID : HID + 2 * HID // DIM].reshape(2, HID),
+        grads[5],
+        grads[6],
     )
 
 

time: 203 us -> 168 us (0.83)
  Pallas kernels: 190 us -> 158 us
  local copies, waits for them, and re-layouts: 10.8 us -> 4.07 us
  other arithmetic: 0.94 us -> 4.76 us
    pallas_call x3 -> x2, Pallas kernels: 190 us -> 158 us  [the longest x1 141 us: step(): pl.pallas_call(step_kernel, out_shape=(jax.ShapeDtypeStruct((ROWS, HID),...]
    reshape x5 -> x0, local copies, waits for them, and re-layouts: 4.67 us -> none  [the longest x1 1.27 us: local(): gain = norm_gain.reshape(1, HID)]
    slice x3 -> x0, local copies, waits for them, and re-layouts: 3.77 us -> none  [the longest x1 1.77 us: local(): side[:HID]]
    reduce_sum x2, other arithmetic: 0.89 us -> 3.97 us  [the longest x1 3.29 us: ask_slots(): rank = jnp.sum((same & earlier).astype(jnp.int32), axis=(2, 3))]
where the time goes in v3:
time: 168 us
  Pallas kernels  158 us (94%)
  other arithmetic  4.76 us (3%)
  local copies, waits for them, and re-layouts  4.07 us (2%)
    pallas_call x1, Pallas kernels, step(): pl.pallas_call(step_kernel, out_shape=(jax.ShapeDtypeStruct((ROWS, HID),...  141 us
    pallas_call x1, Pallas kernels, finish(): pl.pallas_call(finish_kernel, grid=(FFW // wide,), out_shape=(jax.ShapeDt...  17.4 us

profile of v3, /device:TPU:1, one launch (start us, length us, event | category | flops | bytes accessed | tf_op | source)
XLA Modules:
  0.0 167.7 jit_solution(155218392474644919)
XLA Ops:
  0.7 3.3 %convert_reduce_fusion = s32[8,16]{1,0:T(8,128)S(1)} fusion(s32[8,16]{1,0:T(8,128)} %param.18, pred[8,8]{1,0:T(8,128)(4,1)S(1)} %iota_compare_fusion.1), kind=kLoop, calls=%fused_computation | loop fusion | flops 65408 | bytes 1088 | tf_op jit(solution)/shard_map/reduce_sum | solution.py:701
  4.0 0.8 fusion.9
  4.8 0.0 copy-start.3
  4.8 0.7 select_reduce_fusion
  5.5 0.1 add.114
  5.6 0.7 pad.4.codes
  6.3 0.0 copy-done.3
  6.3 140.6 %step.1 = (bf16[1280,768]{1,0:T(8,128)(2,1)}, bf16[3,2,3072,128]{3,2,1,0:T(8,128)(2,1)}, f32[2,512,128]{2,1,0:T(8,128)}, f32[8,128]{1,0:T(8,128)}) custom-call(s32[256]{0:T(256)} %get-tuple-element.33.slot_query, s32[8,16]{1,0:T(8,128)} %copy-done.3, s32[128,1,128]{2,1,0:T(1,128)} %pad.4.codes, bf16[256,3072]{1,0:T(8,128)(2,1)} %bitcast.12, ...), custom_call_target="tpu_custom_call" | custom-call | tf_op jit(solution)/shard_map/step/pallas_call | solution.py:580
  146.9 0.0 copy-start
  146.9 1.5 copy-done
  148.4 0.0 copy-start.1
  148.4 1.0 copy-done.1
  149.5 0.0 copy-start.2
  149.5 0.7 copy-done.2
  150.1 17.4 %finish.1 = (bf16[256,3072]{1,0:T(8,128)(2,1)}, bf16[1024,3072]{1,0:T(8,128)(2,1)}, bf16[256,768]{1,0:T(8,128)(2,1)}, bf16[1024,768]{1,0:T(8,128)(2,1)}, f32[307...) custom-call(bf16[1280,768]{1,0:T(8,128)(2,1)S(1)} %copy-done, bf16[3072,768]{1,0:T(8,128)(2,1)} %weight.1, ...), custom_call_target="tpu_custom_call" | custom-call | tf_op jit(solution)/shard_map/finish/pallas_call | solution.py:654
  (3 shorter events, 0.0 us)
Async XLA Ops:
  4.8 1.5 copy-start.3
  146.9 1.5 copy-start
  148.4 1.0 copy-start.1
  149.5 0.7 copy-start.2

commit v4 on v3

--- a/solution.py
+++ b/solution.py
@@ -42,6 +42,8 @@
 PARTS = 3
 PART_ROWS = 3072
 SIDE_ROWS = 512
+PIECES = [(part, first, rows) for first, rows in ((0, 2048), (2048, 1024)) for part in range(PARTS)]
+PIECES += [(PARTS, 0, SIDE_ROWS)]
 
 
 def position():
@@ -76,6 +78,44 @@
 
 def iota(shape, axis):
     return lax.broadcasted_iota(jnp.int32, shape, axis)
+
+
+def ask_plan(place, owner, index):
+    away = (
+        ((owner // 32 + 4 - place["x"]) % 4) * 32
+        + (((owner // 8) % 4 + 4 - place["z"]) % 4) * 8
+        + (((owner // 4) % 2 + 2 - place["core"]) % 2) * 4
+        + (owner % 4 + 4 - place["y"]) % 4
+    )
+    lane = iota((Q_DEV, DIM), 1)
+    asks = jnp.zeros((Q_DEV, DIM), jnp.int32)
+    asked = jnp.zeros((Q_DEV, DIM), jnp.int32)
+    for k in range(NEG):
+        here = away[:, k : k + 1] == lane
+        asks += jnp.where(here, 1, 0)
+        asked += jnp.where(here, index[:, k : k + 1], 0)
+    seen = jnp.zeros((1, DIM), jnp.int32)
+    ranks = []
+    for i in range(Q_DEV):
+        ranks.append(seen)
+        seen = seen + asks[i : i + 1]
+    rank = jnp.concatenate(ranks, axis=0)
+    slots = jnp.zeros((Q_DEV, DIM), jnp.int32)
+    for k in range(NEG):
+        column = away[:, k : k + 1]
+        found = jnp.sum(jnp.where(column == lane, rank, 0), axis=1, keepdims=True)
+        slots += jnp.where(lane == k, column * CAP + jnp.minimum(found, CAP - 1), 0)
+    query = iota((Q_DEV, DIM), 0)
+    square = iota((DEVICES, DIM), 0) == iota((DEVICES, DIM), 1)
+    rows, columns = [], jnp.zeros((DEVICES, DIM), jnp.int32)
+    for r in range(CAP):
+        mine = (asks == 1) & (rank == r)
+        rows.append(jnp.sum(jnp.where(mine, query, 0), axis=0, keepdims=True))
+        code = Q_DEV + jnp.sum(jnp.where(mine, query * 16 + asked - Q_DEV, 0), axis=0, keepdims=True)
+        column = jnp.sum(jnp.where(square, code, 0), axis=1, keepdims=True)
+        columns += jnp.where(iota((DEVICES, DIM), 1) == r, column, 0)
+    rows += [jnp.zeros((Q_DEV - CAP, DIM), jnp.int32), slots]
+    return jnp.concatenate(rows, axis=0), columns
 
 
 def count_of(mask, axis):
@@ -134,10 +174,10 @@
 
 
 def step_kernel(
-    slot_query, slot_of, codes,
+    owners, indices,
     query_inner, query_resid, passage_inner, passage_resid, out_weight, gain_in, bias_in, proj,
-    grad_summed, out_ref, side_out, loss_out,
-    gain, bias, inner, resid, weight, normed_out, unit_out, scale_out, grad_out,
+    grad_hbm, out_hbm, side_hbm, loss_out,
+    codes, codes_mid, plan, plan_s, grad_summed, out_ref, side_out, gain, bias, inner, resid, weight, normed_out, unit_out, scale_out, grad_out,
     query_emb, passage_emb, codes_in, table, table_s,
     asks_out, asks_in, sorted_q, sorted_w, sorted_pull, sorted_exp, slot_exp, slot_seed, block_seed, chain,
     pulls_out, pulls_in, anchor_w, anchor_pull, anchor_score,
@@ -145,7 +185,7 @@
     grad, side, proj_sum,
     core_in, held, in1, held1, in2, held2, in3,
     score_in, sheld, sin1, sheld1, sin2, sheld2, sin3,
-    load_sem, table_sem, code_send, code_recv, ask_send, ask_recv, pull_send, pull_recv, sum_send, sum_recv,
+    load_sem, table_sem, store_sem, code_send, code_recv, ask_send, ask_recv, pull_send, pull_recv, sum_send, sum_recv,
     send_sem, recv_sem,
 ):
     place = position()
@@ -176,23 +216,32 @@
     sorted_exp[SORTED] = jnp.zeros((1, DIM), f32)
     slot_seed[SLOTS] = jnp.zeros((1, DIM), f32)
     chain[BLOCKS] = jnp.zeros((PLEN, DIM), f32)
-    codes_in[0] = codes[0]
+    plan_rows, code_columns = ask_plan(place, owners[...], indices[...])
+    plan[...] = plan_rows
+    to_plan = pltpu.make_async_copy(plan, plan_s, table_sem)
+    to_plan.start()
+    codes[...] = code_columns.reshape(16, 8, 1, DIM)
+    codes_mid[0] = codes[:, 0]
     gain[...] = gain_in[...].reshape(1, HID)
     bias[...] = bias_in[...].reshape(1, HID)
     proj_sum[...] = jnp.zeros_like(proj_sum)
     pl.semaphore_wait(barrier, DEVICES - 1)
 
-    def code_copy(t):
-        return pltpu.make_async_remote_copy(
-            src_ref=codes.at[t], dst_ref=codes_in.at[t], send_sem=code_send, recv_sem=code_recv,
-            device_id=device_at(offset(place, t, 1)), device_id_type=MESH,
-        )
-
-    def send_code(t, carry):
-        code_copy(t).start()
-        return carry
-
-    lax.fori_loop(1, DEVICES, send_code, 0)
+    code_near, code_far = [], []
+    for t in range(1, 8):
+        peer = shifted(shifted(place, "core", t // 4), "y", t % 4)
+        code_near.append(pltpu.make_async_remote_copy(
+            src_ref=codes.at[:, t], dst_ref=codes_mid.at[t], send_sem=code_send.at[t - 1],
+            recv_sem=code_recv.at[t - 1], device_id=device_at(peer), device_id_type=MESH,
+        ))
+    for t in range(1, 16):
+        peer = shifted(shifted(place, "x", t // 4), "z", t % 4)
+        code_far.append(pltpu.make_async_remote_copy(
+            src_ref=codes_mid.at[:, t], dst_ref=codes_in.at[t], send_sem=code_send.at[t + 6],
+            recv_sem=code_recv.at[t + 6], device_id=device_at(peer), device_id_type=MESH,
+        ))
+    for copy in code_near:
+        copy.start()
 
     def encode(at):
         at = pl.multiple_of(at, CHUNK)
@@ -210,9 +259,15 @@
         scale_out[here, :] = jnp.where(iota((CHUNK, DIM), 1) < DIM // 2, reciprocal, length)
         return unit.astype(bf16)
 
+    to_plan.wait()
     for load in loads[:3]:
         load.wait()
     query_emb[...] = encode(0).reshape(Q_DEV, QLEN, DIM)
+    for copy in code_near:
+        copy.wait_recv()
+    for copy in code_far:
+        copy.start()
+    codes_in[0] = codes_mid[:, 0]
 
     def ask_copy(t):
         rows = pl.ds(t * CAP, CAP)
@@ -221,16 +276,16 @@
             device_id=device_at(offset(place, t, 1)), device_id_type=MESH,
         )
 
-    def take_query(s):
-        return query_emb[slot_query[s]]
+    def take_query(t, r):
+        return query_emb[plan_s[r, t]]
 
     for r in range(CAP):
-        asks_in[r] = take_query(r)
+        asks_in[r] = take_query(0, r)
 
     def send_ask(i, carry):
         t = (i * SPREAD) % DEVICES
         for r in range(CAP):
-            asks_out[t * CAP + r] = take_query(t * CAP + r)
+            asks_out[t * CAP + r] = take_query(t, r)
         ask_copy(t).start()
         return carry
 
@@ -246,12 +301,8 @@
 
     lax.fori_loop(0, P_ROWS // CHUNK, encode_passages, 0)
 
-    rest = pl.ds(1, DEVICES - 1)
-    everyone = pltpu.make_async_remote_copy(
-        src_ref=codes.at[rest], dst_ref=codes_in.at[rest], send_sem=code_send, recv_sem=code_recv,
-        device_id=device_at(offset(place, 1, 1)), device_id_type=MESH,
-    )
-    everyone.wait()
+    for copy in code_far:
+        copy.wait_recv()
     code_rows = codes_in[...].reshape(DEVICES, DIM)
     slot_codes = jnp.concatenate([code_rows[:, r : r + 1] for r in range(CAP)], axis=0)
     table[...] = pair_table(slot_codes)
@@ -349,20 +400,23 @@
     def take_pull(s):
         return sorted_pull[table_s[2, s]]
 
+    for r in range(CAP):
+        pulls_in[r] = take_pull(r)
+
+    def gather_pull(t, carry):
+        for r in range(CAP):
+            pulls_out[t * CAP + r] = take_pull(t * CAP + r)
+        return carry
+
+    lax.fori_loop(1, DEVICES, gather_pull, 0, unroll=2)
     for copy in near:
         copy.wait_recv()
     sums[1] = sums[0] + jnp.sum(sums_in1[...], axis=0)
     for copy in far:
         copy.start()
 
-    for r in range(CAP):
-        pulls_in[r] = take_pull(r)
-
     def send_pull(i, carry):
-        t = (i * SPREAD) % DEVICES
-        for r in range(CAP):
-            pulls_out[t * CAP + r] = take_pull(t * CAP + r)
-        pull_copy(t).start()
+        pull_copy((i * SPREAD) % DEVICES).start()
         return carry
 
     lax.fori_loop(1, DEVICES, send_pull, 0)
@@ -457,11 +511,13 @@
         rows = pl.ds(i * QLEN, QLEN)
         pull = jnp.zeros((QLEN, DIM), f32)
         for k in range(NEG):
-            pull += pulls_in[slot_of[i, k]].astype(f32)
+            pull += pulls_in[plan_s[8 + i, k]].astype(f32)
         grad_out[rows, :] = (
             pull * query_scale[i : i + 1, :] + anchor_pull[rows, :] * anchor_seed[i : i + 1, :]
         )
     norm_sums = back(0, norm_sums)
+    stores = [pltpu.make_async_copy(grad_summed, grad_hbm, store_sem.at[len(PIECES), 0])]
+    stores[0].start()
     side[0] = proj_sum[0:SIDE_ROWS, :]
     side[1] = jnp.zeros((SIDE_ROWS, DIM), f32)
     side[1, 0 : HID - SIDE_ROWS, :] = proj_sum[SIDE_ROWS:HID, :]
@@ -481,95 +537,115 @@
         copy.start()
         copies[phase, part, step] = copy
 
-    def bufs(part):
+    def bufs(piece):
+        part, first, rows = PIECES[piece]
         if part < PARTS:
+            at = lambda n: pl.ds(first // n, rows // n)
             return dict(
-                src=grad.at[part], core_in=core_in.at[part], held=held.at[part],
-                ins=(in1.at[part], in2.at[part], in3.at[part]),
-                helds=(held1.at[part], held2.at[part]), out=out_ref.at[part], rows=PART_ROWS,
+                src=lambda half: grad.at[part, half, at(1)], hbm=lambda half: out_hbm.at[part, half, at(1)],
+                core_in=core_in.at[part, at(1)], held=held.at[part, at(1)],
+                ins=tuple(
+                    (lambda t, ref=ref, n=n: ref.at[part, t, at(n)])
+                    for ref, n in ((in1, 4), (in2, 16), (in3, 64))
+                ),
+                helds=(held1.at[part, at(4)], held2.at[part, at(16)]), out=out_ref.at[part, at(1)], rows=rows,
             )
         return dict(
-            src=side, core_in=score_in, held=sheld, ins=(sin1, sin2, sin3),
-            helds=(sheld1, sheld2), out=side_out, rows=SIDE_ROWS,
+            src=lambda half: side.at[half], hbm=lambda half: side_hbm.at[half], core_in=score_in, held=sheld,
+            ins=tuple((lambda t, ref=ref: ref.at[t]) for ref in (sin1, sin2, sin3)),
+            helds=(sheld1, sheld2), out=side_out, rows=rows,
         )
 
-    every = range(PARTS + 1)
+    every = range(len(PIECES))
+    last = len(PIECES) - 1
 
     def send_half(part):
         b = bufs(part)
-        send(0, part, 0, b["src"].at[other], b["core_in"], shifted(place, "core", 1))
-
-    send_half(PARTS)
+        send(0, part, 0, b["src"](other), b["core_in"], shifted(place, "core", 1))
+
+    send_half(last)
     weights(other, 0, Q_ROWS, True)
-    for part in range(PARTS):
+    for part in range(last):
         send_half(part)
     weights(core, 0, Q_ROWS, True)
 
     for part in every:
         b = bufs(part)
         copies[0, part, 0].wait_recv()
-        add_rows(b["held"], 0, [(b["src"].at[core], 0), (b["core_in"], 0)], b["rows"], 128)
+        add_rows(b["held"], 0, [(b["src"](core), 0), (b["core_in"], 0)], b["rows"], 128)
         rows = b["rows"] // 4
-        axis = ORDERS[part][0]
+        axis = ORDERS[PIECES[part][0]][0]
         for t in (1, 2, 3):
             peer = shifted(place, axis, t)
             at = pl.multiple_of(peer[axis] * rows, rows)
-            send(1, part, t - 1, b["held"].at[pl.ds(at, rows)], b["ins"][0].at[t - 1], peer)
+            send(1, part, t - 1, b["held"].at[pl.ds(at, rows)], b["ins"][0](t - 1), peer)
     for phase in (1, 2, 3):
         for part in every:
             b = bufs(part)
             rows = b["rows"] // 4**phase
-            axis = ORDERS[part][phase - 1]
+            axis = ORDERS[PIECES[part][0]][phase - 1]
             here = b["held"] if phase == 1 else b["helds"][phase - 2]
             for t in (1, 2, 3):
                 copies[phase, part, t - 1].wait_recv()
-            terms = [(here, place[axis] * rows)] + [(b["ins"][phase - 1].at[t], 0) for t in range(3)]
+            terms = [(here, place[axis] * rows)] + [(b["ins"][phase - 1](t), 0) for t in range(3)]
             if phase < 3:
                 target, at = b["helds"][phase - 1], 0
             else:
-                target = b["out"].at[core]
-                at = sum(place[a] * (b["rows"] // 4 ** (n + 1)) for n, a in enumerate(ORDERS[part]))
-            add_rows(target, at, terms, rows, 96 if rows % 96 == 0 else min(rows, 64))
+                target = b["out"]
+                at = sum(place[a] * (b["rows"] // 4 ** (n + 1)) for n, a in enumerate(ORDERS[PIECES[part][0]]))
+            add_rows(target, at, terms, rows, min(rows, 128))
             if phase < 3:
-                axis = ORDERS[part][phase]
+                axis = ORDERS[PIECES[part][0]][phase]
                 rows = rows // 4
                 for t in (1, 2, 3):
                     peer = shifted(place, axis, t)
                     start = pl.multiple_of(peer[axis] * rows, rows)
-                    send(phase + 1, part, t - 1, target.at[pl.ds(start, rows)], b["ins"][phase].at[t - 1], peer)
+                    send(phase + 1, part, t - 1, target.at[pl.ds(start, rows)], b["ins"][phase](t - 1), peer)
             else:
-                axis = ORDERS[part][2]
-                block = target.at[pl.ds(pl.multiple_of(at, 8 if part == PARTS else 16), rows)]
+                axis = ORDERS[PIECES[part][0]][2]
+                block = target.at[pl.ds(pl.multiple_of(at, 8 if part == last else 16), rows)]
                 for t in (1, 2, 3):
                     send(4, part, t - 1, block, block, shifted(place, axis, t))
-    for phase in (4, 5, 6):
+    def hand_over(part, piece, at, rows):
+        b = bufs(part)
+        here = pl.ds(pl.multiple_of(at, rows), rows)
+        send(7, part, piece, b["out"].at[here], b["hbm"](core).at[here], shifted(place, "core", 1))
+        copy = pltpu.make_async_copy(b["out"].at[here], b["hbm"](core).at[here], store_sem.at[part, piece])
+        copy.start()
+        stores.append(copy)
+
+    for phase in (4, 5):
         for part in every:
             b = bufs(part)
             for t in (1, 2, 3):
                 copies[phase, part, t - 1].wait_recv()
-            target = b["out"].at[core]
-            if phase < 6:
-                depth = 6 - phase
-                rows = b["rows"] // 4**depth
-                axis = ORDERS[part][depth - 1]
-                at = sum(
-                    place[a] * (b["rows"] // 4 ** (n + 1)) for n, a in enumerate(ORDERS[part][:depth])
-                )
-                block = target.at[pl.ds(pl.multiple_of(at, 8 if part == PARTS else 16), rows)]
-                for t in (1, 2, 3):
-                    send(phase + 1, part, t - 1, block, block, shifted(place, axis, t))
-            else:
-                send(7, part, 0, target, target, shifted(place, "core", 1))
+            depth = 6 - phase
+            rows = b["rows"] // 4**depth
+            axis = ORDERS[PIECES[part][0]][depth - 1]
+            at = sum(place[a] * (b["rows"] // 4 ** (n + 1)) for n, a in enumerate(ORDERS[PIECES[part][0]][:depth]))
+            block = b["out"].at[pl.ds(pl.multiple_of(at, 8 if part == last else 16), rows)]
+            for t in (1, 2, 3):
+                send(phase + 1, part, t - 1, block, block, shifted(place, axis, t))
+            if phase == 5:
+                hand_over(part, 0, at, rows)
+    for t in (1, 3, 2):
+        for part in every:
+            copies[6, part, t - 1].wait_recv()
+            rows = bufs(part)["rows"] // 4
+            axis = ORDERS[PIECES[part][0]][0]
+            hand_over(part, t, shifted(place, axis, 4 - t)[axis] * rows, rows)
     for part in every:
-        copies[7, part, 0].wait_recv()
+        for piece in range(4):
+            copies[7, part, piece].wait_recv()
     for copy in copies.values():
         copy.wait_send()
-    for copy in near + far:
+    for copy in stores:
+        copy.wait()
+    for copy in code_near + code_far + near + far:
         copy.wait_send()
 
 
-def step(slot_query, slot_of, codes, query_inner, query_resid, passage_inner, passage_resid,
-         out_weight, gain, bias, proj):
+def step(owners, indices, query_inner, query_resid, passage_inner, passage_resid, out_weight, gain, bias, proj):
     any_, vmem, smem = pl.ANY, pltpu.VMEM, pltpu.SMEM
     spec = lambda space: pl.BlockSpec(memory_space=space)
     dma = pltpu.SemaphoreType.DMA
@@ -585,14 +661,17 @@
             jax.ShapeDtypeStruct((2, s, DIM), f32),
             jax.ShapeDtypeStruct((Q_DEV, DIM), f32),
         ),
-        in_specs=[spec(smem), spec(smem), spec(vmem)] + [spec(any_)] * 5 + [spec(vmem)] * 3,
-        out_specs=(spec(vmem),) * 4,
+        in_specs=[spec(vmem)] * 2 + [spec(any_)] * 5 + [spec(vmem)] * 3,
+        out_specs=(spec(any_),) * 3 + (spec(vmem),),
         scratch_shapes=[
+            vmem((16, 8, 1, DIM), jnp.int32), vmem((8, 16, 1, DIM), jnp.int32),
+            vmem((16, DIM), jnp.int32), smem((16, DIM), jnp.int32),
+            vm(ROWS, HID), vm(PARTS, r, DIM), vf(s, DIM),
             vf(1, HID), vf(1, HID),
             vm(ROWS, FFW), vm(ROWS, HID), vm(FFW, HID),
             vf(ROWS, HID), vf(ROWS, DIM), vf(ROWS, DIM), vf(ROWS, DIM),
             vm(Q_DEV, QLEN, DIM), vm(Q_DEV, PLEN, DIM),
-            vmem((DEVICES, 1, DIM), jnp.int32), vmem((8, WIDE), jnp.int32), smem((8, WIDE), jnp.int32),
+            vmem((16, 8, 1, DIM), jnp.int32), vmem((8, WIDE), jnp.int32), smem((8, WIDE), jnp.int32),
             vm(SLOTS, QLEN, DIM), vm(SLOTS + 1, QLEN, DIM),
             vm(SORTED * QLEN, DIM), vm(SORTED * QLEN, DIM), vm(SORTED + 1, QLEN, DIM),
             vf(SORTED + 1, 1, DIM), vf(SLOTS, DIM), vf(SLOTS + 1, 1, DIM), vf(8, DIM),
@@ -605,55 +684,74 @@
             vm(PARTS, 3, r // 16, DIM), vm(PARTS, r // 16, DIM), vm(PARTS, 3, r // 64, DIM),
             vf(s, DIM), vf(s, DIM), vf(3, s // 4, DIM), vf(s // 4, DIM),
             vf(3, s // 16, DIM), vf(s // 16, DIM), vf(3, s // 64, DIM),
-            dma((5,)), dma, dma, dma, dma, dma, dma, dma, dma((22,)), dma((22,)),
-            dma((8, PARTS + 1, 3)), dma((8, PARTS + 1, 3)),
+            dma((5,)), dma, dma((len(PIECES) + 1, 4)), dma((22,)), dma((22,)), dma, dma, dma, dma, dma((22,)), dma((22,)),
+            dma((8, len(PIECES), 4)), dma((8, len(PIECES), 4)),
         ],
         compiler_params=pltpu.CompilerParams(
             collective_id=1, has_side_effects=True, vmem_limit_bytes=63 * MIB
         ),
         name="step",
-    )(slot_query, slot_of, codes, query_inner, query_resid, passage_inner, passage_resid, out_weight,
-      gain, bias, proj)
+    )(owners, indices, query_inner, query_resid, passage_inner, passage_resid, out_weight, gain, bias, proj)
+
+
+FINISH = 6
+WIDE_ROWS = FFW // FINISH
 
 
 def finish_kernel(
-    grad_summed, weight, total, side, loss,
+    grad_hbm, weight_hbm, total_hbm, side, loss,
     query_inner, passage_inner, query_resid, passage_resid, summed, proj_grad, norm_grad, query_loss,
+    grad_summed, weight, total, inner, wide, load_sem, store_sem,
 ):
-    for part in range(PARTS):
-        for h in range(2):
-            column = part * 256 + h * DIM
-            summed[:, column : column + DIM] = total[part, 0, h, 0].astype(f32)
-    query_inner[...] = dot(grad_summed[0:Q_ROWS, :], weight[...], (1, 1)).astype(bf16)
-
-    def block(n, carry):
-        rows = pl.ds(pl.multiple_of(n * CHUNK, CHUNK), CHUNK)
-        from_rows = pl.ds(pl.multiple_of(Q_ROWS + n * CHUNK, CHUNK), CHUNK)
-        passage_inner[rows, :] = dot(grad_summed[from_rows, :], weight[...], (1, 1)).astype(bf16)
-        return carry
-
-    lax.fori_loop(0, P_ROWS // CHUNK, block, 0)
-
-    @pl.when(pl.program_id(0) == 0)
-    def _():
-        query_resid[...] = grad_summed[0:Q_ROWS, :]
-        passage_resid[...] = grad_summed[Q_ROWS:ROWS, :]
-        proj_grad[0:SIDE_ROWS, :] = side[0]
-        proj_grad[SIDE_ROWS:HID, :] = side[1, 0 : HID - SIDE_ROWS, :]
-        for n in range(2):
-            for j in range(HID // DIM):
-                row = HID - SIDE_ROWS + n * (HID // DIM) + j
-                norm_grad[n : n + 1, j * DIM : (j + 1) * DIM] = side[1, row : row + 1, :]
-        for i in range(Q_DEV):
-            query_loss[i] = loss[i, 0]
+    loads = [pltpu.make_async_copy(grad_hbm, grad_summed, load_sem.at[0])]
+    for n in range(FINISH):
+        rows = pl.ds(n * WIDE_ROWS, WIDE_ROWS)
+        loads.append(pltpu.make_async_copy(weight_hbm.at[rows], weight.at[rows], load_sem.at[1 + n]))
+        loads.append(pltpu.make_async_copy(
+            total_hbm.at[:, n // 3, :, n % 3], total.at[n], load_sem.at[1 + FINISH + n]
+        ))
+    for load in loads:
+        load.start()
+    stores = []
+
+    def store(src, dst):
+        copy = pltpu.make_async_copy(src, dst, store_sem.at[len(stores)])
+        copy.start()
+        stores.append(copy)
+
+    proj_grad[0:SIDE_ROWS, :] = side[0]
+    proj_grad[SIDE_ROWS:HID, :] = side[1, 0 : HID - SIDE_ROWS, :]
+    for n in range(2):
+        for j in range(HID // DIM):
+            row = HID - SIDE_ROWS + n * (HID // DIM) + j
+            norm_grad[n : n + 1, j * DIM : (j + 1) * DIM] = side[1, row : row + 1, :]
+    for i in range(Q_DEV):
+        query_loss[i] = loss[i, 0]
+    loads[0].wait()
+    store(grad_summed.at[pl.ds(0, Q_ROWS)], query_resid)
+    store(grad_summed.at[pl.ds(Q_ROWS, P_ROWS)], passage_resid)
+    for n in range(FINISH):
+        rows = pl.ds(n * WIDE_ROWS, WIDE_ROWS)
+        loads[1 + 2 * n].wait()
+
+        inner[:, rows] = dot(grad_summed[...], weight[rows, :], (1, 1)).astype(bf16)
+        store(inner.at[pl.ds(0, Q_ROWS), rows], query_inner.at[:, rows])
+        store(inner.at[pl.ds(Q_ROWS, P_ROWS), rows], passage_inner.at[:, rows])
+        loads[2 + 2 * n].wait()
+        for part in range(PARTS):
+            for h in range(2):
+                column = part * 256 + h * DIM
+                wide[rows, column : column + DIM] = total[n, part, h].astype(f32)
+        store(wide.at[rows], summed.at[rows])
+    for copy in stores:
+        copy.wait()
 
 
 def finish(grad_summed, weight, total, side, loss):
-    wide = 512
-    whole = lambda *shape: pl.BlockSpec(shape, lambda i: (0,) * len(shape))
+    spec = lambda space: pl.BlockSpec(memory_space=space)
+    any_, vmem, smem = pl.ANY, pltpu.VMEM, pltpu.SMEM
     return pl.pallas_call(
         finish_kernel,
-        grid=(FFW // wide,),
         out_shape=(
             jax.ShapeDtypeStruct((Q_ROWS, FFW), bf16),
             jax.ShapeDtypeStruct((P_ROWS, FFW), bf16),
@@ -664,47 +762,20 @@
             jax.ShapeDtypeStruct((2, HID), f32),
             jax.ShapeDtypeStruct((Q_DEV,), f32),
         ),
-        in_specs=[
-            whole(ROWS, HID),
-            pl.BlockSpec((wide, HID), lambda i: (i, 0)),
-            pl.BlockSpec((PARTS, 1, 2, 1, wide, DIM), lambda i: (0, i // 3, 0, i % 3, 0, 0)),
-            whole(2, SIDE_ROWS, DIM),
-            pl.BlockSpec(memory_space=pltpu.SMEM),
+        in_specs=[spec(any_)] * 3 + [spec(vmem), spec(smem)],
+        out_specs=(spec(any_),) * 5 + (spec(vmem), spec(vmem), spec(smem)),
+        scratch_shapes=[
+            vmem((ROWS, HID), bf16),
+            vmem((FFW, HID), bf16),
+            vmem((FINISH, PARTS, 2, WIDE_ROWS, DIM), bf16),
+            vmem((ROWS, FFW), bf16),
+            vmem((FFW, HID), f32),
+            pltpu.SemaphoreType.DMA((1 + 2 * FINISH,)),
+            pltpu.SemaphoreType.DMA((2 + 3 * FINISH,)),
         ],
-        out_specs=(
-            pl.BlockSpec((Q_ROWS, wide), lambda i: (0, i)),
-            pl.BlockSpec((P_ROWS, wide), lambda i: (0, i)),
-            whole(Q_ROWS, HID),
-            whole(P_ROWS, HID),
-            pl.BlockSpec((wide, HID), lambda i: (i, 0)),
-            whole(HID, DIM),
-            whole(2, HID),
-            pl.BlockSpec(memory_space=pltpu.SMEM),
-        ),
-        compiler_params=pltpu.CompilerParams(vmem_limit_bytes=48 * MIB),
+        compiler_params=pltpu.CompilerParams(vmem_limit_bytes=60 * MIB),
         name="finish",
     )(grad_summed, weight, total, side, loss)
-
-
-def ask_slots(negative_owner, negative_index):
-    place = position()
-    owner = negative_owner
-    away = (
-        ((owner // 32 + 4 - place["x"]) % 4) * 32
-        + (((owner // 8) % 4 + 4 - place["z"]) % 4) * 8
-        + (((owner // 4) % 2 + 2 - place["core"]) % 2) * 4
-        + (owner % 4 + 4 - place["y"]) % 4
-    )
-    query = jnp.arange(Q_DEV, dtype=jnp.int32)
-    same = owner[None, None] == owner[:, :, None, None]
-    earlier = query[None, None, :, None] < query[:, None, None, None]
-    rank = jnp.sum((same & earlier).astype(jnp.int32), axis=(2, 3))
-    slot_of = away * CAP + rank
-    hit = slot_of[None] == jnp.arange(SLOTS, dtype=jnp.int32)[:, None, None]
-    slot_query = jnp.sum(jnp.where(hit, query[:, None], 0), axis=(1, 2))
-    codes = Q_DEV + jnp.sum(jnp.where(hit, query[:, None] * 16 + negative_index - Q_DEV, 0), axis=(1, 2))
-    codes = jnp.pad(codes.reshape(DEVICES, 1, CAP), ((0, 0), (0, 0), (0, DIM - CAP)))
-    return slot_query, slot_of, codes
 
 
 def local(
@@ -721,9 +792,8 @@
 ):
     query_inner = query_inner.reshape(Q_ROWS, FFW)
     passage_inner = passage_inner.reshape(P_ROWS, FFW)
-    slot_query, slot_of, codes = ask_slots(negative_owner, negative_index)
     grad_summed, total, side, loss = step(
-        slot_query, slot_of, codes, query_inner, query_resid.reshape(Q_ROWS, HID), passage_inner,
+        negative_owner, negative_index, query_inner, query_resid.reshape(Q_ROWS, HID), passage_inner,
         passage_resid.reshape(P_ROWS, HID), out_weight, norm_gain, norm_bias, proj_weight,
     )
     grads = finish(grad_summed, out_weight, total.reshape(PARTS, 2, 2, 3, 512, DIM), side, loss)

time: 168 us -> 148 us (0.88)
  Pallas kernels: 158 us -> 147 us
  other arithmetic: 4.76 us -> 0 us
  local copies, waits for them, and re-layouts: 4.07 us -> 0 us
    pallas_call x1, Pallas kernels: 141 us -> 134 us  [step(): pl.pallas_call(step_kernel, out_shape=(jax.ShapeDtypeStruct((ROWS, HID),...]
    pallas_call x1, Pallas kernels: 17.4 us -> 13.2 us  [finish(): pl.pallas_call(finish_kernel, out_shape=(jax.ShapeDtypeStruct((Q_ROWS, FF...]
    reduce_sum x2 -> x0, other arithmetic: 3.97 us -> none  [the longest x1 3.29 us: ask_slots(): rank = jnp.sum((same & earlier).astype(jnp.int32), axis=(2, 3))]
    unnamed x8 -> x0, local copies, waits for them, and re-layouts: 3.26 us -> none
where the time goes in v4:
time: 148 us
  Pallas kernels  147 us (99%)
    pallas_call x1, Pallas kernels, step(): pl.pallas_call(step_kernel, out_shape=(jax.ShapeDtypeStruct((ROWS, HID),...  134 us
    pallas_call x1, Pallas kernels, finish(): pl.pallas_call(finish_kernel, out_shape=(jax.ShapeDtypeStruct((Q_ROWS, FF...  13.2 us

profile of v4, /device:TPU:1, one launch (start us, length us, event | category | flops | bytes accessed | tf_op | source)
XLA Modules:
  0.0 148.3 jit_solution(7442040238008275364)
XLA Ops:
  0.6 134.3 %step.1 = (bf16[1280,768]{1,0:T(8,128)(2,1)}, bf16[3,2,3072,128]{3,2,1,0:T(8,128)(2,1)}, f32[2,512,128]{2,1,0:T(8,128)}, f32[8,128]{1,0:T(8,128)}) custom-call(s32[8,16]{1,0:T(8,128)} %owners.1, s32[8,16]{1,0:T(8,128)} %indices.1, bf16[256,3072]{1,0:T(8,128)(2,1)} %bitcast.11, bf16[256,768]{1,0:T(8,128)(2,1)} %bitcast.13, bf16[1024,3072]{1,0:T(8,128)(2,1)} %bitcast.9, ...), custom_call_target="tpu_custom_call" | custom-call | tf_op jit(solution)/shard_map/step/pallas_call | solution.py:656
  134.9 13.2 %finish.1 = (bf16[256,3072]{1,0:T(8,128)(2,1)}, bf16[1024,3072]{1,0:T(8,128)(2,1)}, bf16[256,768]{1,0:T(8,128)(2,1)}, bf16[1024,768]{1,0:T(8,128)(2,1)}, f32[307...) custom-call(bf16[1280,768]{1,0:T(8,128)(2,1)} %get-tuple-element.20.grad_hbm, ...), custom_call_target="tpu_custom_call" | custom-call | tf_op jit(solution)/shard_map/finish/pallas_call | solution.py:753

commit v5 on v4

--- a/solution.py
+++ b/solution.py
@@ -65,10 +65,10 @@
 
 def offset(place, t, sign):
     return {
-        "x": (place["x"] + sign * (t // 32) + 4) % 4,
-        "z": (place["z"] + sign * ((t // 8) % 4) + 4) % 4,
-        "core": (place["core"] + sign * ((t // 4) % 2) + 2) % 2,
-        "y": (place["y"] + sign * (t % 4) + 4) % 4,
+        "x": lax.rem(place["x"] + sign * lax.div(t, 32) + 4, 4),
+        "z": lax.rem(place["z"] + sign * lax.rem(lax.div(t, 8), 4) + 4, 4),
+        "core": lax.rem(place["core"] + sign * lax.rem(lax.div(t, 4), 2) + 2, 2),
+        "y": lax.rem(place["y"] + sign * lax.rem(t, 4) + 4, 4),
     }
 
 
@@ -210,7 +210,7 @@
         pl.semaphore_signal(barrier, inc=1, device_id=device_at(offset(place, t, 1)), device_id_type=MESH)
         return carry
 
-    lax.fori_loop(1, DEVICES, greet, 0)
+    lax.fori_loop(1, DEVICES, greet, 0, unroll=4)
     asks_in[SLOTS] = jnp.zeros((QLEN, DIM), bf16)
     sorted_pull[SORTED] = jnp.zeros((QLEN, DIM), bf16)
     sorted_exp[SORTED] = jnp.zeros((1, DIM), f32)
@@ -283,13 +283,13 @@
         asks_in[r] = take_query(0, r)
 
     def send_ask(i, carry):
-        t = (i * SPREAD) % DEVICES
+        t = lax.rem(i * SPREAD, DEVICES)
         for r in range(CAP):
             asks_out[t * CAP + r] = take_query(t, r)
         ask_copy(t).start()
         return carry
 
-    lax.fori_loop(1, DEVICES, send_ask, 0)
+    lax.fori_loop(1, DEVICES, send_ask, 0, unroll=2)
 
     for load in loads[3:]:
         load.wait()
@@ -326,7 +326,7 @@
 
     all_asks = pltpu.make_async_remote_copy(
         src_ref=asked(asks_out), dst_ref=asked(asks_in), send_sem=ask_send, recv_sem=ask_recv,
-        device_id=device_at(offset(place, 1, 1)), device_id_type=MESH,
+        device_id=device_at(shifted(place, "y", 1)), device_id_type=MESH,
     )
     all_asks.wait()
 
@@ -354,7 +354,7 @@
             slot_exp[pl.ds(r * DEVICES + t, 1), :] = sorted_exp[table_s[2, t * CAP + r]]
         return carry
 
-    lax.fori_loop(0, DEVICES, exp_of, 0)
+    lax.fori_loop(0, DEVICES, exp_of, 0, unroll=4)
 
     t_col = iota((DEVICES, 1), 0)
     source = (
@@ -416,10 +416,10 @@
         copy.start()
 
     def send_pull(i, carry):
-        pull_copy((i * SPREAD) % DEVICES).start()
-        return carry
-
-    lax.fori_loop(1, DEVICES, send_pull, 0)
+        pull_copy(lax.rem(i * SPREAD, DEVICES)).start()
+        return carry
+
+    lax.fori_loop(1, DEVICES, send_pull, 0, unroll=2)
     for copy in far:
         copy.wait_recv()
     total = sums[1] + jnp.sum(sums_in2[...], axis=0)
@@ -504,7 +504,7 @@
 
     pltpu.make_async_remote_copy(
         src_ref=asked(pulls_out), dst_ref=asked(pulls_in), send_sem=pull_send, recv_sem=pull_recv,
-        device_id=device_at(offset(place, 1, 1)), device_id_type=MESH,
+        device_id=device_at(shifted(place, "y", 1)), device_id_type=MESH,
     ).wait()
     query_scale = loss_scale / own_total
     for i in range(Q_DEV):

time: 148 us -> 146 us (0.986)
  Pallas kernels: 147 us -> 145 us
    pallas_call x1, Pallas kernels: 134 us -> 132 us  [step(): pl.pallas_call(step_kernel, out_shape=(jax.ShapeDtypeStruct((ROWS, HID),...]
where the time goes in v5:
time: 146 us
  Pallas kernels  145 us (99%)
    pallas_call x1, Pallas kernels, step(): pl.pallas_call(step_kernel, out_shape=(jax.ShapeDtypeStruct((ROWS, HID),...  132 us
    pallas_call x1, Pallas kernels, finish(): pl.pallas_call(finish_kernel, out_shape=(jax.ShapeDtypeStruct((Q_ROWS, FF...  13.2 us

profile of v5, /device:TPU:1, one launch (start us, length us, event | category | flops | bytes accessed | tf_op | source)
XLA Modules:
  0.0 145.9 jit_solution(17826308315834894537)
XLA Ops:
  0.6 131.9 %step.1 = (bf16[1280,768]{1,0:T(8,128)(2,1)}, bf16[3,2,3072,128]{3,2,1,0:T(8,128)(2,1)}, f32[2,512,128]{2,1,0:T(8,128)}, f32[8,128]{1,0:T(8,128)}) custom-call(s32[8,16]{1,0:T(8,128)} %owners.1, s32[8,16]{1,0:T(8,128)} %indices.1, bf16[256,3072]{1,0:T(8,128)(2,1)} %bitcast.11, bf16[256,768]{1,0:T(8,128)(2,1)} %bitcast.13, bf16[1024,3072]{1,0:T(8,128)(2,1)} %bitcast.9, ...), custom_call_target="tpu_custom_call" | custom-call | tf_op jit(solution)/shard_map/step/pallas_call | solution.py:656
  132.6 13.2 %finish.1 = (bf16[256,3072]{1,0:T(8,128)(2,1)}, bf16[1024,3072]{1,0:T(8,128)(2,1)}, bf16[256,768]{1,0:T(8,128)(2,1)}, bf16[1024,768]{1,0:T(8,128)(2,1)}, f32[307...) custom-call(bf16[1280,768]{1,0:T(8,128)(2,1)} %get-tuple-element.20.grad_hbm, ...), custom_call_target="tpu_custom_call" | custom-call | tf_op jit(solution)/shard_map/finish/pallas_call | solution.py:753
